TPU v7x, 512 devices: a whole 4x4x16 slice. The times are simulated.
512 devices in a mesh: off: 64 (over y, x, z_lo), dep: 8 (over z_hi, core).
Axes of the slice: x: 4, y: 4, z: 16 (z_hi: 4, z_lo: 4; z = z_hi * 4 + z_lo), core: 2. Of those that a mesh axis runs over, the one named last changes fastest.
Arguments:
- snapshots: bfloat16 [64, 32, 64, 256], P('off', 'dep'), may hold values from -6 to 6
- reflect: bfloat16 [768, 32, 64, 256], P('off', 'dep'), may hold values from -0.21875 to 0.21875
- courant: float32 [32, 64, 256], P('dep'), may hold values from 0.03 to 0.18
- lags: int32 [768], P('off'), may hold values from -32 to 32, as said below
- owners: int32 [8], replicated, may hold values from 0 to 63, as said below
Outputs:
- scattered: float32 [32, 64, 256], P('dep')
Inputs may be any that keep to these rules, and one draw needn't show every extreme that they name: `lags`: some offset has lag -32 and some offset has lag 32. `owners`: some step uses wavefield 0 and some step uses wavefield 64 - 1.
All inputs are finite; a program needn't handle non-finite values.
Results may differ from a plain program's by a relative error of at most 0.0003.
Values may be sent and summed in bfloat16 or wider, within the bound.
A program may use at most 64 MiB of HBM per device.

v0:
```python
import jax
import jax.numpy as jnp
from jax import lax
from jax.sharding import PartitionSpec as P

ITERS = 8
LAG = 32


STENCIL_WEIGHTS = (-205.0 / 72.0, 8.0 / 5.0, -1.0 / 5.0, 8.0 / 315.0, -1.0 / 560.0)


def broadcast(x, axis, root):
    mine = lax.axis_index(axis) == root
    return lax.psum(jnp.where(mine, x, jnp.zeros_like(x)), axis)


def extended(cells, sides, width):
    for axis, dim in sides:
        count = lax.axis_size(axis)
        ends = count - 1
        head = lax.slice_in_dim(cells, 0, width, axis=dim)
        tail = lax.slice_in_dim(cells, cells.shape[dim] - width, cells.shape[dim], axis=dim)
        cells = jnp.concatenate(
            [
                lax.ppermute(tail, axis, [(i, (i + 1) % count) for i in range(ends)]),
                cells,
                lax.ppermute(head, axis, [((i + 1) % count, i) for i in range(ends)]),
            ],
            axis=dim,
        )
    return cells


def stencil(padded, depth_cells, row_cells, column_cells):
    center = padded[4 : 4 + depth_cells, 4 : 4 + row_cells, 4 : 4 + column_cells]
    summed = 3.0 * STENCIL_WEIGHTS[0] * center
    for distance in range(1, 5):
        neighbours = (
            padded[
                4 + distance : 4 + distance + depth_cells, 4 : 4 + row_cells, 4 : 4 + column_cells
            ]
            + padded[
                4 - distance : 4 - distance + depth_cells, 4 : 4 + row_cells, 4 : 4 + column_cells
            ]
        )
        neighbours = (
            neighbours
            + padded[
                4 : 4 + depth_cells, 4 + distance : 4 + distance + row_cells, 4 : 4 + column_cells
            ]
            + padded[
                4 : 4 + depth_cells, 4 - distance : 4 - distance + row_cells, 4 : 4 + column_cells
            ]
        )
        neighbours = (
            neighbours
            + padded[
                4 : 4 + depth_cells, 4 : 4 + row_cells, 4 + distance : 4 + distance + column_cells
            ]
            + padded[
                4 : 4 + depth_cells, 4 : 4 + row_cells, 4 - distance : 4 - distance + column_cells
            ]
        )
        summed = summed + STENCIL_WEIGHTS[distance] * neighbours
    return summed


def shifted_sum(reflect, acceleration, lags):
    width_cells = acceleration.shape[2]
    padded = jnp.pad(acceleration, ((0, 0), (0, 0), (LAG, LAG)))

    def add_offset(offset_index, summed):
        lag_now = lags[offset_index]
        window = lax.dynamic_slice_in_dim(padded, LAG - lag_now, width_cells, 2)
        return summed + reflect[offset_index].astype(jnp.float32) * window

    return lax.fori_loop(
        0, reflect.shape[0], add_offset, jnp.zeros(acceleration.shape, jnp.float32)
    )


def accelerate(rimmed, courant):
    padded = jnp.pad(rimmed, ((0, 0), (4, 4), (4, 4))).astype(jnp.float32)
    return courant * stencil(padded, courant.shape[0], courant.shape[1], courant.shape[2])


def per_device(snapshots, reflect, courant, lags, owners):
    depth_cells = courant.shape[0]
    row_cells = courant.shape[1]
    column_cells = courant.shape[2]
    scattered = jnp.zeros((depth_cells, row_cells, column_cells), jnp.float32)
    previous = jnp.zeros((depth_cells, row_cells, column_cells), jnp.float32)
    for step_now in range(ITERS):
        background = broadcast(snapshots[0], "off", owners[step_now])
        rimmed = extended(background, (("dep", 0),), 4)
        acceleration = accelerate(rimmed, courant)
        local_source = shifted_sum(reflect, acceleration, lags)
        source = lax.psum(local_source, "off")
        field_padded = extended(scattered, (("dep", 0),), 4)
        field_padded = jnp.pad(field_padded, ((0, 0), (4, 4), (4, 4)))
        updated = (
            2.0 * scattered
            - previous
            + courant * stencil(field_padded, depth_cells, row_cells, column_cells)
            + source
        )
        previous = scattered
        scattered = updated
    return scattered


def solution(mesh):
    in_specs = (
        P("off", "dep", None, None),
        P("off", "dep", None, None),
        P("dep", None, None),
        P("off"),
        P(),
    )
    out_specs = P("dep", None, None)
    return jax.shard_map(
        per_device, mesh=mesh, in_specs=in_specs, out_specs=out_specs, check_vma=False
    )
```

profile of v0, /device:TPU:1, one launch (start us, length us, event | category | flops | bytes accessed | tf_op | source)
XLA Modules:
  0.0 1998.0 jit_solution(5249608897246558371)
XLA Ops:
  15.1 688.1 %all-reduce.33.cloned.1.call-done = (bf16[4,64,256]{2,1,0:T(8,128)(2,1)}, bf16[4,64,256]{2,1,0:T(8,128)(2,1)}, bf16[4,64,256]{2,1,0:T(8,128)(2,1)}, bf16[4,64,25...) async-done(((bf16[4,64,256]{2,1,0:T(8,128)(2,1)}, ...) | async-done | bytes 1048592 | tf_op jit(solution)/shard_map/psum | solution.py:15
  703.3 45.6 %collective-permute-start.31 = (bf16[4,64,256]{2,1,0:T(8,128)(2,1)}, bf16[4,64,256]{2,1,0:T(8,128)(2,1)S(1)}, u32[]{:S(2)}, u32[]{:S(2)}) collective-permute-start(bf16[4,64,256]{2,1,0:T(8,128)(2,1)} %get-tuple-element.1301), channel_id=1, source_target_pairs={{1,0},{2,1},{3,2},{4,3},{5,4},{6,5},{7,6},{9,8},{10,9},{11,10},{12... | collective-permute-start | bytes 393224 | tf_op jit(solution)/shard_map/ppermute | solution.py:28
  748.9 7.4 collective-permute-start.30
  758.4 7.6 collective-permute-start.26
  767.9 7.6 collective-permute-start.22
  781.4 47.8 %while.135 = (s32[]{:T(128)}, f32[4,64,256]{2,1,0:T(8,128)}, bf16[12,4,64,256]{3,2,1,0:T(8,128)(2,1)S(1)}, s32[12]{0:T(128)S(1)}, f32[4,64,320]{2,1,0:T(8,128)},...) while((s32[]{:T(128)}, f32[4,64,256]{2,1,0:T(8,128)}, ...), condition=%wide.region_30.31_spmd.clone, body=%wide.region_29.30_spmd.clone.sunk | while | flops 262151 | bytes 917681 | solution.py:78
  829.2 7.5 collective-permute-start.18
  842.9 46.3 %while.134 = (s32[]{:T(128)}, f32[4,64,256]{2,1,0:T(8,128)}, bf16[12,4,64,256]{3,2,1,0:T(8,128)(2,1)S(1)}, s32[12]{0:T(128)S(1)}, f32[4,64,320]{2,1,0:T(8,128)},...) while((s32[]{:T(128)}, f32[4,64,256]{2,1,0:T(8,128)}, ...), condition=%wide.region_26.27_spmd.clone, body=%wide.region_25.26_spmd.clone.sunk | while | flops 262151 | bytes 917681 | solution.py:78
  889.2 7.5 collective-permute-start.14
  902.8 37.0 %while.133 = (s32[]{:T(128)}, f32[4,64,256]{2,1,0:T(8,128)S(1)}, bf16[12,4,64,256]{3,2,1,0:T(8,128)(2,1)S(1)}, s32[12]{0:T(128)S(1)}, f32[4,64,320]{2,1,0:T(8,12...) while((s32[]{:T(128)}, f32[4,64,256]{2,1,0:T(8,128)S(1)}, ...), condition=%wide.region_22.23_spmd.clone, body=%wide.region_21.22_spmd.clone.sunk | while | flops 262151 | bytes 917681 | solution.py:78
  939.8 7.6 collective-permute-start.10
  953.4 39.0 %while.132 = (s32[]{:T(128)}, f32[4,64,256]{2,1,0:T(8,128)S(1)}, bf16[12,4,64,256]{3,2,1,0:T(8,128)(2,1)S(1)}, s32[12]{0:T(128)S(1)}, f32[4,64,320]{2,1,0:T(8,12...) while((s32[]{:T(128)}, f32[4,64,256]{2,1,0:T(8,128)S(1)}, ...), condition=%wide.region_18.19_spmd.clone, body=%wide.region_17.18_spmd.clone.sunk | while | flops 262151 | bytes 917681 | solution.py:78
  992.5 7.6 collective-permute-start.6
  1005.5 25.6 %while.131 = (s32[]{:T(128)}, f32[4,64,256]{2,1,0:T(8,128)S(1)}, bf16[12,4,64,256]{3,2,1,0:T(8,128)(2,1)S(1)}, s32[12]{0:T(128)S(1)}, f32[4,64,320]{2,1,0:T(8,12...) while((s32[]{:T(128)}, f32[4,64,256]{2,1,0:T(8,128)S(1)}, ...), condition=%wide.region_14.15_spmd.clone, body=%wide.region_13.14_spmd.clone.sunk | while | flops 262151 | bytes 917681 | solution.py:78
  1031.1 7.5 collective-permute-start.2
  1042.1 26.1 %while.130 = (s32[]{:T(128)}, f32[4,64,256]{2,1,0:T(8,128)S(1)}, bf16[12,4,64,256]{3,2,1,0:T(8,128)(2,1)S(1)}, s32[12]{0:T(128)S(1)}, f32[4,64,320]{2,1,0:T(8,12...) while((s32[]{:T(128)}, f32[4,64,256]{2,1,0:T(8,128)S(1)}, ...), condition=%wide.region_10.11_spmd.clone, body=%wide.region_9.10_spmd.clone.sunk | while | flops 262151 | bytes 917681 | solution.py:78
  1071.7 27.6 %while.129 = (s32[]{:T(128)}, f32[4,64,256]{2,1,0:T(8,128)S(1)}, bf16[12,4,64,256]{3,2,1,0:T(8,128)(2,1)S(1)}, s32[12]{0:T(128)S(1)}, f32[4,64,320]{2,1,0:T(8,12...) while((s32[]{:T(128)}, f32[4,64,256]{2,1,0:T(8,128)S(1)}, ...), condition=%wide.region_6.7_spmd.clone, body=%wide.region_5.6_spmd.clone.sunk | while | flops 262151 | bytes 917681 | solution.py:78
  1102.7 25.2 %while.128 = (s32[]{:T(128)}, f32[4,64,256]{2,1,0:T(8,128)S(1)}, bf16[12,4,64,256]{3,2,1,0:T(8,128)(2,1)S(1)}, s32[12]{0:T(128)S(1)}, f32[4,64,320]{2,1,0:T(8,12...) while((s32[]{:T(128)}, f32[4,64,256]{2,1,0:T(8,128)S(1)}, ...), condition=%wide.region_2.3_spmd.clone, body=%wide.region_1.2_spmd.clone.sunk | while | flops 262151 | bytes 917681 | solution.py:78
  1130.6 7.5 collective-permute-start.1
  1138.2 7.9 collective-permute-done
  1146.5 668.9 %all-reduce.31.cloned.1.call-done = (f32[4,64,256]{2,1,0:T(8,128)}, f32[4,64,256]{2,1,0:T(8,128)}, f32[4,64,256]{2,1,0:T(8,128)}, f32[4,64,256]{2,1,0:T(8,128)},...) async-done(((f32[4,64,256]{2,1,0:T(8,128)}, f32[4,64,256]{2,1,0:T(8,128)}, f32[4,64,256]{2,1,0:T(8,128)}, ...) | async-done | bytes 2097168 | tf_op jit(solution)/shard_map/psum | solution.py:99
  1817.5 50.1 %collective-permute-start.5 = (f32[4,64,256]{2,1,0:T(8,128)S(1)}, f32[4,64,256]{2,1,0:T(8,128)S(1)}, u32[]{:S(2)}, u32[]{:S(2)}) collective-permute-start(f32[4,64,256]{2,1,0:T(8,128)S(1)} %fusion.191), channel_id=1, source_target_pairs={{0,1},{1,2},{2,3},{3,4},{4,5},{5,6},{6,7},{8,9},{9,10},{10,11},{11... | collective-permute-start | bytes 786440 | tf_op jit(solution)/shard_map/ppermute | solution.py:26
  1871.0 13.8 collective-permute-done.4
  1888.5 2.4 collective-permute-start.8
  1891.7 11.9 collective-permute-done.8
  1907.3 2.4 collective-permute-start.12
  1910.6 11.2 collective-permute-done.12
  1928.7 10.0 collective-permute-done.16
  1942.4 2.4 collective-permute-start.20
  1945.7 8.9 collective-permute-done.20
  1961.5 9.6 collective-permute-done.24
  1978.0 10.9 collective-permute-done.28
  (323 shorter events, 238.9 us)
Async XLA Ops:
  6.5 696.8 %all-reduce.33.cloned.1.call-start = ((), (), s32[]{:S(2)}) async-start(), calls=%async_computation.1 | async-start | bytes 2097152 | tf_op jit(solution)/shard_map/psum | solution.py:15
  15.1 1800.4 %all-reduce.31.cloned.1.call-start = ((), (), s32[]{:S(2)}) async-start(), calls=%async_computation | async-start | bytes 4194304 | tf_op jit(solution)/shard_map/psum | solution.py:99
  703.3 64.6 %collective-permute-start.31 = (bf16[4,64,256]{2,1,0:T(8,128)(2,1)}, bf16[4,64,256]{2,1,0:T(8,128)(2,1)S(1)}, u32[]{:S(2)}, u32[]{:S(2)}) collective-permute-start(bf16[4,64,256]{2,1,0:T(8,128)(2,1)} %get-tuple-element.1301), channel_id=1, source_target_pairs={{1,0},{2,1},{3,2},{4,3},{5,4},{6,5},{7,6},{9,8},{10,9},{11,10},{12... | collective-permute-start | bytes 393224 | tf_op jit(solution)/shard_map/ppermute | solution.py:28
  748.9 26.5 %collective-permute-start.30 = (bf16[4,64,256]{2,1,0:T(8,128)(2,1)}, bf16[4,64,256]{2,1,0:T(8,128)(2,1)S(1)}, u32[]{:S(2)}, u32[]{:S(2)}) collective-permute-start(bf16[4,64,256]{2,1,0:T(8,128)(2,1)} %get-tuple-element.1301), channel_id=1, source_target_pairs={{0,1},{1,2},{2,3},{3,4},{4,5},{5,6},{6,7},{8,9},{9,10},{10,11},{11... | collective-permute-start | bytes 393224 | tf_op jit(solution)/shard_map/ppermute | solution.py:26
  756.4 72.8 %collective-permute-start.27 = (bf16[4,64,256]{2,1,0:T(8,128)(2,1)}, bf16[4,64,256]{2,1,0:T(8,128)(2,1)}, u32[]{:S(2)}, u32[]{:S(2)}) collective-permute-start(bf16[4,64,256]{2,1,0:T(8,128)(2,1)} %get-tuple-element.1302), channel_id=1, source_target_pairs={{1,0},{2,1},{3,2},{4,3},{5,4},{6,5},{7,6},{9,8},{10,9},{11,10},{12... | collective-permute-start | bytes 393224 | tf_op jit(solution)/shard_map/ppermute | solution.py:28
  758.4 78.4 %collective-permute-start.26 = (bf16[4,64,256]{2,1,0:T(8,128)(2,1)}, bf16[4,64,256]{2,1,0:T(8,128)(2,1)}, u32[]{:S(2)}, u32[]{:S(2)}) collective-permute-start(bf16[4,64,256]{2,1,0:T(8,128)(2,1)} %get-tuple-element.1302), channel_id=1, source_target_pairs={{0,1},{1,2},{2,3},{3,4},{4,5},{5,6},{6,7},{8,9},{9,10},{10,11},{11... | collective-permute-start | bytes 393224 | tf_op jit(solution)/shard_map/ppermute | solution.py:26
  765.9 123.2 %collective-permute-start.23 = (bf16[4,64,256]{2,1,0:T(8,128)(2,1)}, bf16[4,64,256]{2,1,0:T(8,128)(2,1)}, u32[]{:S(2)}, u32[]{:S(2)}) collective-permute-start(bf16[4,64,256]{2,1,0:T(8,128)(2,1)} %get-tuple-element.1303), channel_id=1, source_target_pairs={{1,0},{2,1},{3,2},{4,3},{5,4},{6,5},{7,6},{9,8},{10,9},{11,10},{12... | collective-permute-start | bytes 393224 | tf_op jit(solution)/shard_map/ppermute | solution.py:28
  767.9 128.9 %collective-permute-start.22 = (bf16[4,64,256]{2,1,0:T(8,128)(2,1)}, bf16[4,64,256]{2,1,0:T(8,128)(2,1)}, u32[]{:S(2)}, u32[]{:S(2)}) collective-permute-start(bf16[4,64,256]{2,1,0:T(8,128)(2,1)} %get-tuple-element.1303), channel_id=1, source_target_pairs={{0,1},{1,2},{2,3},{3,4},{4,5},{5,6},{6,7},{8,9},{9,10},{10,11},{11... | collective-permute-start | bytes 393224 | tf_op jit(solution)/shard_map/ppermute | solution.py:26
  775.4 164.3 %collective-permute-start.19 = (bf16[4,64,256]{2,1,0:T(8,128)(2,1)}, bf16[4,64,256]{2,1,0:T(8,128)(2,1)}, u32[]{:S(2)}, u32[]{:S(2)}) collective-permute-start(bf16[4,64,256]{2,1,0:T(8,128)(2,1)} %get-tuple-element.1304), channel_id=1, source_target_pairs={{1,0},{2,1},{3,2},{4,3},{5,4},{6,5},{7,6},{9,8},{10,9},{11,10},{12... | collective-permute-start | bytes 393224 | tf_op jit(solution)/shard_map/ppermute | solution.py:28
  829.2 118.1 %collective-permute-start.18 = (bf16[4,64,256]{2,1,0:T(8,128)(2,1)}, bf16[4,64,256]{2,1,0:T(8,128)(2,1)}, u32[]{:S(2)}, u32[]{:S(2)}) collective-permute-start(bf16[4,64,256]{2,1,0:T(8,128)(2,1)} %get-tuple-element.1304), channel_id=1, source_target_pairs={{0,1},{1,2},{2,3},{3,4},{4,5},{5,6},{6,7},{8,9},{9,10},{10,11},{11... | collective-permute-start | bytes 393224 | tf_op jit(solution)/shard_map/ppermute | solution.py:26
  836.8 155.7 %collective-permute-start.15 = (bf16[4,64,256]{2,1,0:T(8,128)(2,1)S(1)}, bf16[4,64,256]{2,1,0:T(8,128)(2,1)}, u32[]{:S(2)}, u32[]{:S(2)}) collective-permute-start(bf16[4,64,256]{2,1,0:T(8,128)(2,1)S(1)} %copy-done.15), channel_id=1, source_target_pairs={{1,0},{2,1},{3,2},{4,3},{5,4},{6,5},{7,6},{9,8},{10,9},{11,10},{12... | collective-permute-start | bytes 393224 | tf_op jit(solution)/shard_map/ppermute | solution.py:28
  889.2 110.9 %collective-permute-start.14 = (bf16[4,64,256]{2,1,0:T(8,128)(2,1)S(1)}, bf16[4,64,256]{2,1,0:T(8,128)(2,1)}, u32[]{:S(2)}, u32[]{:S(2)}) collective-permute-start(bf16[4,64,256]{2,1,0:T(8,128)(2,1)S(1)} %copy-done.15), channel_id=1, source_target_pairs={{0,1},{1,2},{2,3},{3,4},{4,5},{5,6},{6,7},{8,9},{9,10},{10,11},{11... | collective-permute-start | bytes 393224 | tf_op jit(solution)/shard_map/ppermute | solution.py:26
  896.7 134.4 %collective-permute-start.11 = (bf16[4,64,256]{2,1,0:T(8,128)(2,1)}, bf16[4,64,256]{2,1,0:T(8,128)(2,1)}, u32[]{:S(2)}, u32[]{:S(2)}) collective-permute-start(bf16[4,64,256]{2,1,0:T(8,128)(2,1)} %get-tuple-element.1306), channel_id=1, source_target_pairs={{1,0},{2,1},{3,2},{4,3},{5,4},{6,5},{7,6},{9,8},{10,9},{11,10},{12... | collective-permute-start | bytes 393224 | tf_op jit(solution)/shard_map/ppermute | solution.py:28
  939.8 98.9 %collective-permute-start.10 = (bf16[4,64,256]{2,1,0:T(8,128)(2,1)}, bf16[4,64,256]{2,1,0:T(8,128)(2,1)}, u32[]{:S(2)}, u32[]{:S(2)}) collective-permute-start(bf16[4,64,256]{2,1,0:T(8,128)(2,1)} %get-tuple-element.1306), channel_id=1, source_target_pairs={{0,1},{1,2},{2,3},{3,4},{4,5},{5,6},{6,7},{8,9},{9,10},{10,11},{11... | collective-permute-start | bytes 393224 | tf_op jit(solution)/shard_map/ppermute | solution.py:26
  947.3 120.8 %collective-permute-start.7 = (bf16[4,64,256]{2,1,0:T(8,128)(2,1)}, bf16[4,64,256]{2,1,0:T(8,128)(2,1)}, u32[]{:S(2)}, u32[]{:S(2)}) collective-permute-start(bf16[4,64,256]{2,1,0:T(8,128)(2,1)} %get-tuple-element.1307), channel_id=1, source_target_pairs={{1,0},{2,1},{3,2},{4,3},{5,4},{6,5},{7,6},{9,8},{10,9},{11,10},{12... | collective-permute-start | bytes 393224 | tf_op jit(solution)/shard_map/ppermute | solution.py:28
  992.5 75.7 %collective-permute-start.6 = (bf16[4,64,256]{2,1,0:T(8,128)(2,1)}, bf16[4,64,256]{2,1,0:T(8,128)(2,1)}, u32[]{:S(2)}, u32[]{:S(2)}) collective-permute-start(bf16[4,64,256]{2,1,0:T(8,128)(2,1)} %get-tuple-element.1307), channel_id=1, source_target_pairs={{0,1},{1,2},{2,3},{3,4},{4,5},{5,6},{6,7},{8,9},{9,10},{10,11},{11... | collective-permute-start | bytes 393224 | tf_op jit(solution)/shard_map/ppermute | solution.py:26
  1000.0 99.2 %collective-permute-start.3 = (bf16[4,64,256]{2,1,0:T(8,128)(2,1)}, bf16[4,64,256]{2,1,0:T(8,128)(2,1)}, u32[]{:S(2)}, u32[]{:S(2)}) collective-permute-start(bf16[4,64,256]{2,1,0:T(8,128)(2,1)} %get-tuple-element.1308), channel_id=1, source_target_pairs={{1,0},{2,1},{3,2},{4,3},{5,4},{6,5},{7,6},{9,8},{10,9},{11,10},{12... | collective-permute-start | bytes 393224 | tf_op jit(solution)/shard_map/ppermute | solution.py:28
  1031.1 68.2 %collective-permute-start.2 = (bf16[4,64,256]{2,1,0:T(8,128)(2,1)}, bf16[4,64,256]{2,1,0:T(8,128)(2,1)S(1)}, u32[]{:S(2)}, u32[]{:S(2)}) collective-permute-start(bf16[4,64,256]{2,1,0:T(8,128)(2,1)} %get-tuple-element.1308), channel_id=1, source_target_pairs={{0,1},{1,2},{2,3},{3,4},{4,5},{5,6},{6,7},{8,9},{9,10},{10,11},{11... | collective-permute-start | bytes 393224 | tf_op jit(solution)/shard_map/ppermute | solution.py:26
  1128.7 17.4 collective-permute-start
  1130.6 15.4 collective-permute-start.1
  1817.5 53.5 %collective-permute-start.5 = (f32[4,64,256]{2,1,0:T(8,128)S(1)}, f32[4,64,256]{2,1,0:T(8,128)S(1)}, u32[]{:S(2)}, u32[]{:S(2)}) collective-permute-start(f32[4,64,256]{2,1,0:T(8,128)S(1)} %fusion.191), channel_id=1, source_target_pairs={{0,1},{1,2},{2,3},{3,4},{4,5},{5,6},{6,7},{8,9},{9,10},{10,11},{11... | collective-permute-start | bytes 786440 | tf_op jit(solution)/shard_map/ppermute | solution.py:26
  1867.6 17.2 collective-permute-start.4
  1886.4 5.4 collective-permute-start.9
  1888.5 15.2 collective-permute-start.8
  1905.2 5.4 collective-permute-start.13
  1907.3 14.5 collective-permute-start.12
  1925.4 13.3 collective-permute-start.16
  1940.3 5.4 collective-permute-start.21
  1942.4 12.2 collective-permute-start.20
  1956.1 5.4 collective-permute-start.25
  1958.2 12.9 collective-permute-start.24
  1974.7 14.2 collective-permute-start.28
  (19 other events, 1043.9 us)
Sparse Core Ops, SparseCore 0:
  15.2 688.0 all-reduce.32
  1128.8 686.6 all-reduce.30
where the time goes:
time: 2010 us; the launch traced here: 2000 us
  waiting for transfers between devices  1450 us (72%)
  starting transfers between devices  208 us (10%)
  loops' own time  128 us (6%)
  other arithmetic  127 us (6%)
  local copies, waits for them, and re-layouts  68.1 us (3%)
    psum x1, waiting for transfers between devices, broadcast(): return lax.psum(jnp.where(mine, x, jnp.zeros_like(x)), axis)  688 us
    psum x1, waiting for transfers between devices, per_device(): source = lax.psum(local_source, 'off')  669 us
    ppermute x16, starting transfers between devices, extended(): lax.ppermute(tail, axis, [(i, (i + 1) % count) for i in range(ends)])  130 us
    another operation x8, loops' own time, shifted_sum(): lax.fori_loop(0, reflect.shape[0], add_offset, jnp.zeros(acceleration.sha...  128 us
    add x96, other arithmetic, add_offset(): return summed + reflect[offset_index].astype(jnp.float32) * window  85.8 us
    ppermute x16, waiting for transfers between devices, extended(): lax.ppermute(head, axis, [((i + 1) % count, i) for i in range(ends)])  84.4 us
    ppermute x16, starting transfers between devices, extended(): lax.ppermute(head, axis, [((i + 1) % count, i) for i in range(ends)])  77.8 us
    dynamic_slice x96, local copies, waits for them, and re-layouts, add_offset(): lag_now = lags[offset_index]  61.4 us
  transfers between devices with their start and end apart: 34, of which 17 were waited for; matrix products, arithmetic and copies ran while one was open for 8% of the time, Pallas kernels for 0%

commit v1 on v0

v1 whole, which is shorter than its diff:
```python
import jax
import jax.numpy as jnp
from jax import lax
from jax.experimental import pallas as pl
from jax.experimental.pallas import tpu as pltpu
from jax.sharding import PartitionSpec as P

ITERS = 8
LAG = 32
WEIGHTS = (-205.0 / 72.0, 8.0 / 5.0, -1.0 / 5.0, 8.0 / 315.0, -1.0 / 560.0)
MESH = pl.DeviceIdType.MESH
F32 = jnp.float32
BF16 = jnp.bfloat16
OFFSETS = 12
CHUNKS = 3
PART = OFFSETS // CHUNKS


def rem(a, n):
    return lax.rem(a, jnp.int32(n))


def div(a, n):
    return lax.div(a, jnp.int32(n))


def block_of(xy):
    y, x = div(xy, 4), rem(xy, 4)
    return 4 * y + x + rem(y, 2) * (3 - 2 * x)


def column_of(block):
    return block_of(block)


def quarter_of(block, z):
    return z + rem(block, 2) * (3 - 2 * z)


def device_of(piece):
    block = div(piece, 4)
    return column_of(block) * 4 + quarter_of(block, rem(piece, 4))


def transposed(identity, matrix):
    return lax.dot_general(identity, matrix, (((1,), (1,)), ((), ())), preferred_element_type=F32)


def laplace(cur, left, right, up, down):
    row = lax.broadcasted_iota(jnp.int32, (8, 128), 0)
    lane = lax.broadcasted_iota(jnp.int32, (8, 128), 1)
    cell = rem(row, 4)
    line = rem(lane, 64)
    low = lane < 64
    turned = lambda v: pltpu.roll(v, 64, 1)
    swapped_cur = pltpu.roll(cur, 4, 0)
    ahead = jnp.where(row < 4, swapped_cur, pltpu.roll(down, 4, 0))
    behind = jnp.where(row >= 4, swapped_cur, pltpu.roll(up, 4, 0))
    t_cur, t_ahead, t_behind = turned(cur), turned(ahead), turned(behind)
    t_up, t_down = turned(up), turned(down)
    depth = {
        1: jnp.where(low, t_cur, t_ahead) + jnp.where(low, t_behind, t_cur),
        2: ahead + behind,
        3: jnp.where(low, t_ahead, t_down) + jnp.where(low, t_up, t_behind),
        4: up + down,
    }
    total = (3.0 * WEIGHTS[0]) * cur
    for k in range(1, 5):
        near = depth[k]
        near = near + jnp.where(line < 64 - k, pltpu.roll(cur, 128 - k, 1), 0.0)
        near = near + jnp.where(line >= k, pltpu.roll(cur, k, 1), 0.0)
        if k < 4:
            near = near + jnp.where(cell < 4 - k, pltpu.roll(cur, 8 - k, 0), pltpu.roll(right, 4 - k, 0))
            near = near + jnp.where(cell >= k, pltpu.roll(cur, k, 0), pltpu.roll(left, 4 + k, 0))
        else:
            near = near + right + left
        total = total + WEIGHTS[k] * near
    return total


def kernel(
    snap_hbm, refl_hbm, cour_hbm, lags_ref, owners_ref, out_ref,
    snap_v, refl_v, cour_v, load_sem,
    snap_t, snap_r, snap_ss, snap_rs,
    refl_t, refl_r, refl_ss, refl_rs, own_sem,
    lag_v, lag_r, lag_s, lag_ss, lag_rs, lag_sem,
    pick_s, pick_r, pick_ss, pick_rs,
    back_s, back_r, back_ss, back_rs,
    acc_z, acc_zss, acc_zrs,
    acc, acc_ss, acc_rs,
    sum_s, sum_r, sum_ss, sum_rs,
    wave_s, wave_r, wave_ss, wave_rs,
    last_z, last_zss, last_zrs,
    last, last_ss, last_rs,
):
    off = lax.axis_index("off")
    dep = lax.axis_index("dep")
    z, xy = rem(off, 4), div(off, 4)
    y, x = div(xy, 4), rem(xy, 4)
    block = block_of(xy)
    quarter = quarter_of(block, z)
    piece = 4 * block + quarter

    loads = [
        pltpu.make_async_copy(snap_hbm, snap_v, load_sem.at[0]),
        pltpu.make_async_copy(refl_hbm, refl_v, load_sem.at[1]),
        pltpu.make_async_copy(cour_hbm, cour_v, load_sem.at[2]),
    ]
    for load in loads:
        load.start()

    def column_ahead(k):
        return rem(y + div(k, 4), 4) * 4 + rem(x + rem(k, 4), 4)

    def column_behind(k):
        return rem(y + 4 - div(k, 4), 4) * 4 + rem(x + 4 - rem(k, 4), 4)

    def in_plane(column):
        return {"off": column * 4 + z, "dep": dep}

    def in_column(z_to):
        return {"off": xy * 4 + z_to, "dep": dep}

    left, right = device_of(rem(piece + 63, 64)), device_of(rem(piece + 1, 64))
    up, down = rem(dep + 7, 8), rem(dep + 1, 8)
    sides = [
        {"off": right, "dep": dep},
        {"off": left, "dep": dep},
        {"off": off, "dep": down},
        {"off": off, "dep": up},
    ]
    inside = [
        jnp.where(piece > 0, 1.0, 0.0).astype(F32),
        jnp.where(piece < 63, 1.0, 0.0).astype(F32),
        jnp.where(dep > 0, 1.0, 0.0).astype(F32),
        jnp.where(dep < 7, 1.0, 0.0).astype(F32),
    ]

    def remote(src, dst, send, recv, to):
        return pltpu.make_async_remote_copy(
            src_ref=src, dst_ref=dst, send_sem=send, recv_sem=recv, device_id=to, device_id_type=MESH
        )

    def each(lower, upper, body):
        def run(i, carry):
            body(i)
            return carry

        lax.fori_loop(lower, upper, run, 0)

    barrier = pltpu.get_barrier_semaphore()

    def greet(to):
        pl.semaphore_signal(barrier, inc=1, device_id=to, device_id_type=MESH)

    each(1, 16, lambda k: greet(in_plane(column_ahead(k))))
    for k in range(1, 4):
        greet(in_column(rem(z + k, 4)))
    greet(sides[2])
    greet(sides[3])

    lane = lax.broadcasted_iota(jnp.int32, (8, 128), 1)
    lag_row = jnp.zeros((8, 128), jnp.int32)
    for h in range(OFFSETS):
        lag_row = jnp.where(lane == h, lags_ref[h], lag_row)
    lag_v[...] = lag_row
    lag_r[pl.ds(xy, 1)] = lag_row[None]

    identity = jnp.where(
        lax.broadcasted_iota(jnp.int32, (256, 256), 0) == lax.broadcasted_iota(jnp.int32, (256, 256), 1), 1.0, 0.0
    ).astype(BF16)

    loads[0].wait()
    flipped = transposed(identity, snap_v[...]).astype(BF16)
    snap_t[0] = flipped[:, :128]
    snap_t[1] = flipped[:, 128:]

    pl.semaphore_wait(barrier, 20)

    def slab(column):
        return pl.ds(pl.multiple_of(16 * block_of(column), 16), 16)

    def snap_copy(k, to, slot):
        return remote(snap_t.at[:, slab(to), :], snap_r.at[slot], snap_ss.at[k], snap_rs.at[k], in_plane(to))

    def lag_copy(k, to, slot):
        return remote(lag_v, lag_r.at[slot], lag_ss.at[k], lag_rs.at[k], in_plane(to))

    def refl_copy(part, k, to, slot):
        return remote(
            refl_t.at[pl.ds(part * PART, PART), :, slab(to), :],
            refl_r.at[slot, pl.ds(part * PART, PART)],
            refl_ss.at[part, k],
            refl_rs.at[part, k],
            in_plane(to),
        )

    each(1, 16, lambda k: snap_copy(k, column_ahead(k), xy).start())
    snap_r[pl.ds(xy, 1)] = snap_t[:, slab(xy), :][None]

    loads[1].wait()

    def flip_one(h):
        image = transposed(identity, refl_v[h]).astype(BF16)
        refl_t[h, 0] = image[:, :128]
        refl_t[h, 1] = image[:, 128:]

    for part in range(CHUNKS):
        each(part * PART, (part + 1) * PART, flip_one)
        each(1, 16, lambda k: refl_copy(part, k, column_ahead(k), xy).start())
    each(1, 16, lambda k: lag_copy(k, column_ahead(k), xy).start())
    own = pltpu.make_async_copy(refl_t.at[:, :, slab(xy), :], refl_r.at[xy], own_sem)
    own.start()

    loads[2].wait()
    piece_row = lax.broadcasted_iota(jnp.int32, (8, 256), 0)
    piece_col = lax.broadcasted_iota(jnp.int32, (8, 256), 1)
    courant = jnp.zeros((8, 128), F32)
    for half in range(2):
        chosen = jnp.where(
            (piece_col == 4 * piece + piece_row - 4 * half) & (div(piece_row, 4) == half), 1.0, 0.0
        ).astype(BF16)
        rest = cour_v[pl.ds(128 * half, 128), :]
        for _ in range(3):
            head = rest.astype(BF16)
            rest = rest - head.astype(F32)
            courant = courant + transposed(chosen, head)

    each(1, 16, lambda k: snap_copy(k, xy, column_behind(k)).wait_recv())
    quarters = [[] for _ in range(4)]
    for t in range(ITERS):
        owner = owners_ref[t]
        kept = jnp.where(rem(owner, 4) == z, 1.0, 0.0).astype(F32)
        field = snap_r[div(owner, 4)].astype(F32) * kept
        for q in range(4):
            quarters[q].append(field[0, 4 * q : 4 * q + 4])
            quarters[q].append(field[1, 4 * q : 4 * q + 4])
    for q in range(4):
        pick_s[q] = jnp.concatenate(quarters[q], axis=0).astype(BF16)

    def pick_copy(k):
        z_to = rem(z + k, 4)
        return remote(
            pick_s.at[quarter_of(block, z_to)], pick_r.at[k - 1], pick_ss.at[k - 1], pick_rs.at[k - 1], in_column(z_to)
        )

    for k in range(1, 4):
        pick_copy(k).start()
    back = pick_s[quarter].astype(F32)
    for k in range(1, 4):
        pick_copy(k).wait_recv()
        back = back + pick_r[k - 1].astype(F32)
    back_s[...] = back.astype(BF16)

    def back_copy(side):
        return remote(back_s, back_r.at[side], back_ss.at[side], back_rs.at[side], sides[side])

    for side in range(4):
        back_copy(side).start()
    for side in range(4):
        back_copy(side).wait_recv()

    def accelerate(pair):
        rows = pl.ds(pl.multiple_of(16 * pair, 16), 16)
        cur = back_s[rows, :].astype(F32)
        rim = [back_r[side, rows, :].astype(F32) * inside[side] for side in range(4)]
        for half in range(2):
            part = slice(8 * half, 8 * half + 8)
            value = courant * laplace(cur[part], *[v[part] for v in rim])
            acc_z[quarter, 2 * pair + half] = value

    each(0, ITERS // 2, accelerate)

    def acc_zcopy(k, slot):
        return remote(acc_z.at[slot], acc_z.at[slot], acc_zss.at[k - 1], acc_zrs.at[k - 1], in_column(rem(z + k, 4)))

    for k in range(1, 4):
        acc_zcopy(k, quarter).start()
    for k in range(1, 4):
        acc_zcopy(k, quarter_of(block, rem(z + 4 - k, 4))).wait_recv()

    def gather_acc(t):
        parts = [acc_z[q, t] for q in range(4)]
        for half in range(2):
            acc[t, half, 32:48, :] = jnp.concatenate([v[4 * half : 4 * half + 4] for v in parts], axis=0)

    each(0, ITERS, gather_acc)

    def acc_copy(i, step):
        to = column_of(rem(block + 16 + step, 16))
        return remote(
            acc.at[:, :, 32:48, :], acc.at[:, :, 16 * (2 - step) : 16 * (2 - step) + 16, :],
            acc_ss.at[i], acc_rs.at[i], in_plane(to),
        )

    steps = (1, -1, 2, -2)
    for i, step in enumerate(steps):
        acc_copy(i, step).start()
    own.wait()
    each(1, 16, lambda k: lag_copy(k, xy, column_behind(k)).wait_recv())
    lag_copy_s = pltpu.make_async_copy(lag_r, lag_s, lag_sem)
    lag_copy_s.start()
    lag_copy_s.wait()
    for part in range(CHUNKS):
        each(1, 16, lambda k: refl_copy(part, k, xy, column_behind(k)).wait_recv())
    for i, step in enumerate(steps):
        acc_copy(i, step).wait_recv()
    for i, step in enumerate(steps):

        @pl.when((block - step < 0) | (block - step > 15))
        def _():
            def clear(t):
                for half in range(2):
                    acc[t, half, 16 * (2 - step) : 16 * (2 - step) + 16, :] = jnp.zeros((16, 128), F32)

            each(0, ITERS, clear)

    for half in range(2):

        def add_device(s, sums):
            sums = list(sums)
            for h in range(OFFSETS):
                image = refl_r[s, h, half].astype(F32)
                start = LAG - lag_s[s, 0, h]
                for t in range(ITERS):
                    sums[t] = sums[t] + image * acc[t, half, pl.ds(start, 16), :]
            return tuple(sums)

        sums = lax.fori_loop(0, 16, add_device, tuple(jnp.zeros((16, 128), F32) for _ in range(ITERS)))
        for t in range(ITERS):
            for q in range(4):
                sum_s[q, t, 4 * half : 4 * half + 4, :] = sums[t][4 * q : 4 * q + 4]

    def sum_copy(k):
        z_to = rem(z + k, 4)
        return remote(
            sum_s.at[quarter_of(block, z_to)], sum_r.at[k - 1], sum_ss.at[k - 1], sum_rs.at[k - 1], in_column(z_to)
        )

    for k in range(1, 4):
        sum_copy(k).start()
    for k in range(1, 4):
        sum_copy(k).wait_recv()

    def source(t):
        return sum_s[quarter, t] + sum_r[0, t] + sum_r[1, t] + sum_r[2, t]

    def wave_copy(t, side):
        return remote(
            wave_s.at[t], wave_r.at[t, side], wave_ss.at[t, side], wave_rs.at[t, side], sides[side]
        )

    def advance(t, carry):
        cur, previous = carry
        wave_s[t - 1] = cur
        for side in range(4):
            wave_copy(t - 1, side).start()
        ready = 2.0 * cur - previous + source(t)
        for side in range(4):
            wave_copy(t - 1, side).wait_recv()
        rim = [wave_r[t - 1, side] * inside[side] for side in range(4)]
        return ready + courant * laplace(cur, *rim), cur

    wave, _ = lax.fori_loop(1, ITERS, advance, (source(0), jnp.zeros((8, 128), F32)))

    last_z[pl.ds(quarter, 1)] = wave[None]

    def last_zcopy(k, slot):
        return remote(last_z.at[slot], last_z.at[slot], last_zss.at[k - 1], last_zrs.at[k - 1], in_column(rem(z + k, 4)))

    for k in range(1, 4):
        last_zcopy(k, quarter).start()
    for k in range(1, 4):
        last_zcopy(k, quarter_of(block, rem(z + 4 - k, 4))).wait_recv()
    parts = [last_z[q] for q in range(4)]
    for half in range(2):
        last[half, slab(xy), :] = jnp.concatenate([v[4 * half : 4 * half + 4] for v in parts], axis=0)

    def last_copy(k, to, column):
        rows = slab(column)
        return remote(last.at[:, rows, :], last.at[:, rows, :], last_ss.at[k], last_rs.at[k], in_plane(to))

    each(1, 16, lambda k: last_copy(k, column_ahead(k), xy).start())
    each(1, 16, lambda k: last_copy(k, xy, column_behind(k)).wait_recv())
    for half in range(2):
        out_ref[pl.ds(128 * half, 128), :] = last[half].T

    each(1, 16, lambda k: snap_copy(k, column_ahead(k), xy).wait_send())
    each(1, 16, lambda k: lag_copy(k, column_ahead(k), xy).wait_send())
    for part in range(CHUNKS):
        each(1, 16, lambda k: refl_copy(part, k, column_ahead(k), xy).wait_send())
    for k in range(1, 4):
        pick_copy(k).wait_send()
        acc_zcopy(k, quarter).wait_send()
        sum_copy(k).wait_send()
        last_zcopy(k, quarter).wait_send()
    for side in range(4):
        back_copy(side).wait_send()
        each(0, ITERS - 1, lambda t: wave_copy(t, side).wait_send())
    for i, step in enumerate(steps):
        acc_copy(i, step).wait_send()
    each(1, 16, lambda k: last_copy(k, column_ahead(k), xy).wait_send())


def per_device(snapshots, reflect, courant, lags, owners):
    depth, rows, columns = courant.shape
    lines = depth * rows
    dma = pltpu.SemaphoreType.DMA
    any_space = pl.BlockSpec(memory_space=pl.ANY)
    scalars = pl.BlockSpec(memory_space=pltpu.SMEM)
    out = pl.pallas_call(
        kernel,
        out_shape=jax.ShapeDtypeStruct((lines, columns), F32),
        in_specs=[any_space, any_space, any_space, scalars, scalars],
        out_specs=pl.BlockSpec(memory_space=pltpu.VMEM),
        scratch_shapes=[
            pltpu.VMEM((256, 256), BF16), pltpu.VMEM((OFFSETS, 256, 256), BF16), pltpu.VMEM((256, 256), F32), dma((3,)),
            pltpu.VMEM((2, 256, 128), BF16), pltpu.VMEM((16, 2, 16, 128), BF16), dma((16,)), dma((16,)),
            pltpu.VMEM((OFFSETS, 2, 256, 128), BF16), pltpu.VMEM((16, OFFSETS, 2, 16, 128), BF16),
            dma((CHUNKS, 16)), dma((CHUNKS, 16)), dma,
            pltpu.VMEM((8, 128), jnp.int32), pltpu.VMEM((16, 8, 128), jnp.int32), pltpu.SMEM((16, 8, 128), jnp.int32),
            dma((16,)), dma((16,)), dma,
            pltpu.VMEM((4, 64, 128), BF16), pltpu.VMEM((3, 64, 128), BF16), dma((3,)), dma((3,)),
            pltpu.VMEM((64, 128), BF16), pltpu.VMEM((4, 64, 128), BF16), dma((4,)), dma((4,)),
            pltpu.VMEM((4, ITERS, 8, 128), F32), dma((3,)), dma((3,)),
            pltpu.VMEM((ITERS, 2, 80, 128), F32), dma((4,)), dma((4,)),
            pltpu.VMEM((4, ITERS, 8, 128), F32), pltpu.VMEM((3, ITERS, 8, 128), F32), dma((3,)), dma((3,)),
            pltpu.VMEM((ITERS - 1, 8, 128), F32), pltpu.VMEM((ITERS - 1, 4, 8, 128), F32),
            dma((ITERS - 1, 4)), dma((ITERS - 1, 4)),
            pltpu.VMEM((4, 8, 128), F32), dma((3,)), dma((3,)),
            pltpu.VMEM((2, 256, 128), F32), dma((16,)), dma((16,)),
        ],
        compiler_params=pltpu.CompilerParams(
            collective_id=0, has_side_effects=True, vmem_limit_bytes=32 * 1024 * 1024
        ),
        name="born",
    )(
        snapshots.reshape(lines, columns),
        reflect.reshape(reflect.shape[0], lines, columns),
        courant.reshape(lines, columns),
        lags,
        owners,
    )
    return out.reshape(courant.shape)


def solution(mesh):
    in_specs = (
        P("off", "dep", None, None),
        P("off", "dep", None, None),
        P("dep", None, None),
        P("off"),
        P(),
    )
    return jax.shard_map(
        per_device, mesh=mesh, in_specs=in_specs, out_specs=P("dep", None, None), check_vma=False
    )
```

time: 2010 us -> 105 us (0.05)
  waiting for transfers between devices: 1450 us -> 0 us
  starting transfers between devices: 208 us -> 0 us
  loops' own time: 128 us -> 0 us
  other arithmetic: 127 us -> 0 us
  Pallas kernels: 0 us -> 99.5 us
  local copies, waits for them, and re-layouts: 68.1 us -> 5.28 us
    psum x2 -> x0, waiting for transfers between devices: 1360 us -> none  [the longest x1 688 us: broadcast(): return lax.psum(jnp.where(mine, x, jnp.zeros_like(x)), axis)]
    ppermute x32 -> x0, starting transfers between devices: 208 us -> none  [the longest x16 130 us: extended(): lax.ppermute(tail, axis, [(i, (i + 1) % count) for i in range(ends)])]
    another operation x8 -> x0, loops' own time: 128 us -> none  [shifted_sum(): lax.fori_loop(0, reflect.shape[0], add_offset, jnp.zeros(acceleration.sha...]
    pallas_call x0 -> x1, Pallas kernels: none -> 99.5 us  [per_device(): pl.pallas_call(kernel, out_shape=jax.ShapeDtypeStruct((lines, columns), F...]
    add x104 -> x0, other arithmetic: 96.2 us -> none  [the longest x96 85.8 us: add_offset(): return summed + reflect[offset_index].astype(jnp.float32) * window]
    ppermute x32 -> x0, waiting for transfers between devices: 90.8 us -> none  [the longest x16 84.4 us: extended(): lax.ppermute(head, axis, [((i + 1) % count, i) for i in range(ends)])]
    dynamic_slice x96 -> x0, local copies, waits for them, and re-layouts: 61.4 us -> none  [add_offset(): lag_now = lags[offset_index]]
  transfers between devices with their start and end apart: 34 -> 0, of which waited for: 17 -> 0; matrix products, arithmetic and copies ran while one was open for 8% -> 0% of each run, Pallas kernels for 0% -> 0%
where the time goes in v1:
time: 105 us
  Pallas kernels  99.5 us (95%)
  local copies, waits for them, and re-layouts  5.28 us (5%)
    pallas_call x1, Pallas kernels, per_device(): pl.pallas_call(kernel, out_shape=jax.ShapeDtypeStruct((lines, columns), F...  99.5 us
    unnamed x11, local copies, waits for them, and re-layouts  5.28 us

profile of v1, /device:TPU:1, one launch (start us, length us, event | category | flops | bytes accessed | tf_op | source)
XLA Modules:
  0.0 104.8 jit_solution(5625580574563036356)
XLA Ops:
  0.0 0.0 copy-start
  0.0 1.4 %copy-done = bf16[12,4,64,256]{3,2,1,0:T(8,128)(2,1)S(1)} copy-done((bf16[12,4,64,256]{3,2,1,0:T(8,128)(2,1)S(1)}, bf16[12,4,64,256]{3,2,1,0:T(8,128)(2,1)}, u32[]{:S(2)}) %copy-start) | copy-done | bytes 1572888
  1.4 0.0 copy-start.1
  1.4 0.9 copy-done.1
  2.4 0.0 copy-start.2
  2.4 0.9 copy-done.2
  3.3 0.0 copy-start.3
  3.3 0.7 copy-done.3
  3.9 0.0 copy-start.4
  3.9 0.7 copy-done.4
  4.6 99.5 %born.1 = f32[256,256]{1,0:T(8,128)S(1)} custom-call(bf16[256,256]{1,0:T(8,128)(2,1)S(1)} %bitcast.7, bf16[12,256,256]{2,1,0:T(8,128)(2,1)S(1)} %bitcast.4, f32[256,256]{1,0:T(8,128)S(1)} %bitcast.6, s32[12]{0:T(128)S(1)} %copy-done.3, s32[8]{0:T(128)S(1)} %copy-done.4), custom_call_target="tpu_custom_call" | custom-call | tf_op jit(solution)/shard_map/born/pallas_call | solution.py:411
  104.1 0.7 copy.7
Async XLA Ops:
  0.0 1.4 %copy-start = (bf16[12,4,64,256]{3,2,1,0:T(8,128)(2,1)S(1)}, bf16[12,4,64,256]{3,2,1,0:T(8,128)(2,1)}, u32[]{:S(2)}) copy-start(bf16[12,4,64,256]{3,2,1,0:T(8,128)(2,1)} %param.6) | copy-start | bytes 4718596
  1.4 0.9 copy-start.1
  2.4 0.9 copy-start.2
  3.3 0.7 copy-start.3
  3.9 0.7 copy-start.4

commit v2 on v1

v2 whole, which is shorter than its diff:
```python
import jax
import jax.numpy as jnp
from jax import lax
from jax.experimental import pallas as pl
from jax.experimental.pallas import tpu as pltpu
from jax.sharding import PartitionSpec as P

ITERS = 8
LAG = 32
WEIGHTS = (-205.0 / 72.0, 8.0 / 5.0, -1.0 / 5.0, 8.0 / 315.0, -1.0 / 560.0)
MESH = pl.DeviceIdType.MESH
F32 = jnp.float32
BF16 = jnp.bfloat16
OFFSETS = 12
CHUNKS = 3
PART = OFFSETS // CHUNKS
FIRST = 3
STAR = ((-1, 0), (1, 0), (0, -1), (0, 1))
FAR = ((-2, 0), (2, 0), (0, -2), (0, 2), (-1, -1), (-1, 1), (1, -1), (1, 1))
NEAR = STAR + FAR
ROUNDS = 4


def rem(a, n):
    return lax.rem(a, jnp.int32(n))


def div(a, n):
    return lax.div(a, jnp.int32(n))


def snake(i):
    y, x = div(i, 4), rem(i, 4)
    return 4 * y + x + rem(y, 2) * (3 - 2 * x)


def laplace(cur, prev, nxt, up, down):
    row = lax.broadcasted_iota(jnp.int32, (8, 128), 0)
    line = rem(row, 4)
    halves = lambda v: (v[:8], v[8:])
    turned = lambda v: pltpu.roll(v, 4, 0)
    (u0, u1), (c0, c1), (d0, d1) = halves(up), halves(cur), halves(down)
    tu0, tu1, tc0, tc1, td0, td1 = [turned(v) for v in (u0, u1, c0, c1, d0, d1)]
    join = lambda a, b: jnp.where(row < 4, a, b)
    uu, uc, cc, cd, dd = join(tu0, tu1), join(tu1, tc0), join(tc0, tc1), join(tc1, td0), join(td0, td1)
    depth = (
        {1: cc + uc, 2: c1 + u1, 3: cd + uu, 4: d0 + u0},
        {1: cd + cc, 2: d0 + c0, 3: dd + uc, 4: d1 + u1},
    )
    out = []
    for half in range(2):
        c, p, n = halves(cur)[half], halves(prev)[half], halves(nxt)[half]
        total = (3.0 * WEIGHTS[0]) * c
        for k in range(1, 5):
            near = depth[half][k] + pltpu.roll(c, 128 - k, 1) + pltpu.roll(c, k, 1)
            if k < 4:
                near = near + jnp.where(line < 4 - k, pltpu.roll(c, 8 - k, 0), pltpu.roll(n, 4 - k, 0))
                near = near + jnp.where(line >= k, pltpu.roll(c, k, 0), pltpu.roll(p, 4 + k, 0))
            else:
                near = near + n + p
            total = total + WEIGHTS[k] * near
        out.append(total)
    return jnp.concatenate(out, axis=0)


def windows(field):
    first, second = field[:, :128], field[:, 128:]
    lane = lax.broadcasted_iota(jnp.int32, first.shape, 1)
    f32, s32 = pltpu.roll(first, 32, 1), pltpu.roll(second, 32, 1)
    f96, s96 = pltpu.roll(first, 96, 1), pltpu.roll(second, 96, 1)
    return (
        jnp.where(lane < 32, 0.0, f32),
        jnp.where(lane < 96, f96, s96),
        jnp.where(lane < 32, f32, s32),
        jnp.where(lane < 96, s96, 0.0),
    )


def packed(top, bottom):
    lane = lax.broadcasted_iota(jnp.int32, top.shape, 1)
    return jnp.where(lane < 64, pltpu.roll(top, 96, 1), pltpu.roll(bottom, 32, 1))


def unpacked(a, b):
    lane = lax.broadcasted_iota(jnp.int32, a.shape, 1)
    return jnp.where(lane < 64, a, pltpu.roll(b, 64, 1)), jnp.where(lane < 64, pltpu.roll(a, 64, 1), b)


def kernel(
    snap_hbm, refl_hbm, cour_hbm, lags_ref, owners_ref, out_ref,
    snap_v, refl_v, cour_v, load_sem,
    snap_t, snap_r, snap_ss, snap_rs,
    refl_t, refl_r, refl_ss, refl_rs, own_sem,
    lag_v, lag_r, lag_s, lag_ss, lag_rs, lag_sem,
    cour_w, cour_s, cour_r, cour_ss, cour_rs,
    pick_s, pick_r, pick_ss, pick_rs,
    back_s, back_r, back_ss, back_rs,
    acc_w, acc_z, acc_zss, acc_zrs, moved,
    sum_s, sum_r, sum_ss, sum_rs,
    wave_s, wave_r, wave_f, wave_ss, wave_rs,
    last_z, last_zss, last_zrs,
    last, last_ss, last_rs,
):
    off = lax.axis_index("off")
    dep = lax.axis_index("dep")
    z, xy = rem(off, 4), div(off, 4)
    y, x = div(xy, 4), rem(xy, 4)
    block = snake(xy)

    loads = [
        pltpu.make_async_copy(snap_hbm, snap_v, load_sem.at[0]),
        pltpu.make_async_copy(refl_hbm, refl_v, load_sem.at[1]),
        pltpu.make_async_copy(cour_hbm, cour_v, load_sem.at[2]),
    ]
    for load in loads:
        load.start()

    def column_ahead(k):
        return rem(y + div(k, 4), 4) * 4 + rem(x + rem(k, 4), 4)

    def column_behind(k):
        return rem(y + 4 - div(k, 4), 4) * 4 + rem(x + 4 - rem(k, 4), 4)

    def in_plane(column):
        return {"off": column * 4 + z, "dep": dep}

    def in_column(z_to):
        return {"off": xy * 4 + z_to, "dep": dep}

    def beside(place):
        rows, layers = place
        return {"off": snake(rem(block + 16 + rows, 16)) * 4 + z, "dep": rem(dep + 8 + layers, 8)}

    def inside(place):
        b, d = block + place[0], dep + place[1]
        return jnp.where((b >= 0) & (b < 16) & (d >= 0) & (d < 8), 1.0, 0.0).astype(F32)

    def against(place):
        return (-place[0], -place[1])

    def remote(src, dst, send, recv, to):
        return pltpu.make_async_remote_copy(
            src_ref=src, dst_ref=dst, send_sem=send, recv_sem=recv, device_id=to, device_id_type=MESH
        )

    def each(lower, upper, body):
        def run(i, carry):
            body(i)
            return carry

        lax.fori_loop(lower, upper, run, 0)

    barrier = pltpu.get_barrier_semaphore()

    def greet(to):
        pl.semaphore_signal(barrier, inc=1, device_id=to, device_id_type=MESH)

    each(1, 16, lambda k: greet(in_plane(column_ahead(k))))
    for k in range(1, 4):
        greet(in_column(rem(z + k, 4)))
    met = [place for place in NEAR if place[1] != 0]
    for place in met:
        greet(beside(place))

    lane = lax.broadcasted_iota(jnp.int32, (8, 128), 1)
    lag_row = jnp.zeros((8, 128), jnp.int32)
    for h in range(OFFSETS):
        lag_row = jnp.where(lane == h, lags_ref[h], lag_row)
    lag_v[...] = lag_row
    lag_r[pl.ds(xy, 1)] = lag_row[None]

    to_row = lax.broadcasted_iota(jnp.int32, (256, 256), 0)
    from_row = lax.broadcasted_iota(jnp.int32, (256, 256), 1)
    wanted = rem(div(to_row, 4), 4) * 64 + div(to_row, 16) * 4 + rem(to_row, 4)
    order = jnp.where(from_row == wanted, 1.0, 0.0).astype(BF16)

    def ordered(image):
        return jnp.dot(order, image, preferred_element_type=F32).astype(BF16).reshape(16, 16, 256)

    loads[0].wait()
    snap_t[...] = ordered(snap_v[...])

    pl.semaphore_wait(barrier, 18 + len(met))
    def snap_copy(k, to, slot):
        return remote(snap_t.at[snake(to)], snap_r.at[slot], snap_ss.at[k], snap_rs.at[k], in_plane(to))

    def lag_copy(k, to, slot):
        return remote(lag_v, lag_r.at[slot], lag_ss.at[k], lag_rs.at[k], in_plane(to))

    def refl_copy(part, k, to, slot):
        return remote(
            refl_t.at[snake(to), pl.ds(part * PART, PART)],
            refl_r.at[slot, pl.ds(part * PART, PART)],
            refl_ss.at[part, k],
            refl_rs.at[part, k],
            in_plane(to),
        )

    each(1, 16, lambda k: snap_copy(k, column_ahead(k), xy).start())
    snap_r[pl.ds(xy, 1)] = snap_t[pl.ds(block, 1)]
    loads[1].wait()

    def order_one(h):
        refl_t[:, pl.ds(h, 1)] = ordered(refl_v[h])[:, None]

    for part in range(CHUNKS):
        each(part * PART, (part + 1) * PART, order_one)
        each(1, 16, lambda k: refl_copy(part, k, column_ahead(k), xy).start())
    each(1, 16, lambda k: lag_copy(k, column_ahead(k), xy).start())
    own = pltpu.make_async_copy(refl_t.at[block], refl_r.at[xy], own_sem)
    own.start()
    loads[2].wait()
    odd = rem(block, 2)
    layers = []
    for layer in range(4):
        rows = cour_v[layer, pl.ds(pl.multiple_of(8 * div(block, 2), 8), 8), :]
        layers.append(jnp.where(odd == 0, rows[:4], rows[4:]))
    for q, window in enumerate(windows(jnp.concatenate(layers, axis=0))):
        cour_w[q] = window
    courant = cour_w[z]
    cour_s[...] = courant

    def cour_copy(i):
        return remote(cour_s, cour_r.at[i], cour_ss.at[i], cour_rs.at[i], beside(against(STAR[i])))

    for i in range(4):
        cour_copy(i).start()
    each(1, 16, lambda k: snap_copy(k, xy, column_behind(k)).wait_recv())
    for t in range(ITERS):
        owner = owners_ref[t]
        kept = jnp.where(rem(owner, 4) == z, 1.0, 0.0).astype(F32)
        field = snap_r[div(owner, 4)].astype(F32) * kept
        for q, window in enumerate(windows(field)):
            pick_s[q, 16 * t : 16 * t + 16, :] = window.astype(BF16)

    def pick_copy(k):
        z_to = rem(z + k, 4)
        return remote(pick_s.at[z_to], pick_r.at[k - 1], pick_ss.at[k - 1], pick_rs.at[k - 1], in_column(z_to))

    for k in range(1, 4):
        pick_copy(k).start()
    back = pick_s[z].astype(F32)
    for k in range(1, 4):
        pick_copy(k).wait_recv()
        back = back + pick_r[k - 1].astype(F32)
    back_s[...] = back.astype(BF16)
    def back_copy(i):
        return remote(back_s, back_r.at[i], back_ss.at[i], back_rs.at[i], beside(against(STAR[i])))

    for i in range(4):
        back_copy(i).start()
    for i in range(4):
        back_copy(i).wait_recv()

    def accelerate(t):
        rows = pl.ds(pl.multiple_of(16 * t, 16), 16)
        rim = [back_r[i, rows, :].astype(F32) * inside(STAR[i]) for i in range(4)]
        acc_w[rows, :] = courant * laplace(back_s[rows, :].astype(F32), *rim)

    each(0, ITERS, accelerate)
    acc_z[pl.ds(z, 1)] = packed(acc_w[:64, :], acc_w[64:, :])[None]
    def acc_zcopy(k, slot):
        return remote(acc_z.at[slot], acc_z.at[slot], acc_zss.at[k - 1], acc_zrs.at[k - 1], in_column(rem(z + k, 4)))

    for k in range(1, 4):
        acc_zcopy(k, z).start()
    for k in range(1, 4):
        acc_zcopy(k, rem(z + 4 - k, 4)).wait_recv()
    wide = lax.broadcasted_iota(jnp.int32, (64, 128), 1)
    for side in range(2):
        a = unpacked(acc_z[0], acc_z[1])[side]
        b = unpacked(acc_z[2], acc_z[3])[side]
        rows = slice(64 * side, 64 * side + 64)

        def move_right(lag):
            ra, rb = pltpu.roll(a, lag, 1), pltpu.roll(b, lag, 1)
            moved[LAG + lag, rows, :128] = jnp.where(wide < lag, 0.0, ra)
            moved[LAG + lag, rows, 128:] = jnp.where(wide < lag, ra, rb)

        def move_left(lag):
            ra, rb = pltpu.roll(a, 128 - lag, 1), pltpu.roll(b, 128 - lag, 1)
            moved[LAG - lag, rows, :128] = jnp.where(wide < 128 - lag, ra, rb)
            moved[LAG - lag, rows, 128:] = jnp.where(wide < 128 - lag, rb, 0.0)

        each(0, LAG + 1, move_right)
        each(1, LAG + 1, move_left)
    own.wait()
    each(1, 16, lambda k: lag_copy(k, xy, column_behind(k)).wait_recv())
    scalars = pltpu.make_async_copy(lag_r, lag_s, lag_sem)
    scalars.start()
    scalars.wait()
    sums = tuple(jnp.zeros((16, 256), F32) for _ in range(ITERS))
    for part in range(CHUNKS):
        each(1, 16, lambda k: refl_copy(part, k, xy, column_behind(k)).wait_recv())

        def add_device(s, sums):
            sums = list(sums)
            for h in range(part * PART, (part + 1) * PART):
                image = refl_r[s, h].astype(F32)
                place = lag_s[s, 0, h] + LAG
                for t in range(ITERS):
                    sums[t] = sums[t] + image * moved[place, 16 * t : 16 * t + 16, :]
            return tuple(sums)

        sums = lax.fori_loop(0, 16, add_device, sums)
    for t in range(ITERS):
        for q, window in enumerate(windows(sums[t])):
            sum_s[q, 16 * t : 16 * t + 16, :] = window
    spans = ((0, 16 * FIRST), (16 * FIRST, 16 * (ITERS - FIRST)))

    def sum_copy(i, k):
        z_to = rem(z + k, 4)
        rows = pl.ds(*spans[i])
        return remote(
            sum_s.at[z_to, rows, :], sum_r.at[k - 1, rows, :], sum_ss.at[i, k - 1], sum_rs.at[i, k - 1], in_column(z_to)
        )

    for i in range(2):
        for k in range(1, 4):
            sum_copy(i, k).start()
    for k in range(1, 4):
        sum_copy(0, k).wait_recv()

    def source(t):
        rows = slice(16 * t, 16 * t + 16)
        return sum_s[z, rows, :] + sum_r[0, rows, :] + sum_r[1, rows, :] + sum_r[2, rows, :]

    for i in range(4):
        cour_copy(i).wait_recv()

    def wave_copy(r, i):
        to = beside(against(NEAR[i]))
        if i < 4:
            return remote(wave_s.at[r], wave_r.at[r, i], wave_ss.at[r, i], wave_rs.at[r, i], to)
        return remote(wave_s.at[r, 0], wave_f.at[r, i - 4], wave_ss.at[r, i], wave_rs.at[r, i], to)

    def sent(r):
        return range(len(NEAR) if r < ROUNDS - 1 else 4)

    def at(a, b):
        return (a[0] + b[0], a[1] + b[1])

    old = {place: jnp.zeros((16, 128), F32) for place in ((0, 0),) + STAR}
    wave = source(0)
    masks = {place: inside(place) for place in NEAR}
    courants = {(0, 0): courant}
    for i, place in enumerate(STAR):
        courants[place] = cour_r[i]
    for r in range(ROUNDS):
        wave_s[r, 0] = wave
        if r == 1:
            for k in range(1, 4):
                sum_copy(1, k).wait_recv()
        now = source(2 * r + 1)
        if r < ROUNDS - 1:
            wave_s[r, 1] = now
        for i in sent(r):
            wave_copy(r, i).start()
        field = {(0, 0): wave}
        for i in sent(r):
            wave_copy(r, i).wait_recv()
            place = NEAR[i]
            field[place] = (wave_r[r, i, 0] if i < 4 else wave_f[r, i - 4]) * masks[place]
        ahead = {}
        for place in ((0, 0),) + (STAR if r < ROUNDS - 1 else ()):
            rim = [field[at(place, side)] for side in STAR]
            term = now if place == (0, 0) else wave_r[r, STAR.index(place), 1]
            value = 2.0 * field[place] - old[place] + courants[place] * laplace(field[place], *rim) + term
            ahead[place] = value if place == (0, 0) else value * masks[place]
        if r == ROUNDS - 1:
            wave = ahead[(0, 0)]
            break
        rim = [ahead[side] for side in STAR]
        wave = 2.0 * ahead[(0, 0)] - wave + courant * laplace(ahead[(0, 0)], *rim) + source(2 * r + 2)
        old = ahead
    last_z[pl.ds(z, 1)] = packed(wave[:8], wave[8:])[None]

    def last_zcopy(k, slot):
        return remote(last_z.at[slot], last_z.at[slot], last_zss.at[k - 1], last_zrs.at[k - 1], in_column(rem(z + k, 4)))

    for k in range(1, 4):
        last_zcopy(k, z).start()
    for k in range(1, 4):
        last_zcopy(k, rem(z + 4 - k, 4)).wait_recv()
    west, east = unpacked(last_z[0], last_z[1]), unpacked(last_z[2], last_z[3])
    slab = jnp.concatenate([jnp.concatenate([west[i], east[i]], axis=1) for i in range(2)], axis=0)
    last[pl.ds(block, 1)] = slab[None]

    def last_copy(k, to, column):
        place = snake(column)
        return remote(last.at[place], last.at[place], last_ss.at[k], last_rs.at[k], in_plane(to))

    each(1, 16, lambda k: last_copy(k, column_ahead(k), xy).start())
    each(1, 16, lambda k: last_copy(k, xy, column_behind(k)).wait_recv())
    for layer in range(4):
        for pair in range(8):
            out_ref[layer, 8 * pair : 8 * pair + 8, :] = jnp.concatenate(
                [last[2 * pair + i, 4 * layer : 4 * layer + 4, :] for i in range(2)], axis=0
            )
    each(1, 16, lambda k: snap_copy(k, column_ahead(k), xy).wait_send())
    each(1, 16, lambda k: lag_copy(k, column_ahead(k), xy).wait_send())
    for part in range(CHUNKS):
        each(1, 16, lambda k: refl_copy(part, k, column_ahead(k), xy).wait_send())
    for k in range(1, 4):
        pick_copy(k).wait_send()
        acc_zcopy(k, z).wait_send()
        sum_copy(0, k).wait_send()
        sum_copy(1, k).wait_send()
        last_zcopy(k, z).wait_send()
    for i in range(4):
        back_copy(i).wait_send()
        cour_copy(i).wait_send()
    for r in range(ROUNDS):
        for i in sent(r):
            wave_copy(r, i).wait_send()
    each(1, 16, lambda k: last_copy(k, column_ahead(k), xy).wait_send())


def per_device(snapshots, reflect, courant, lags, owners):
    depth, rows, columns = courant.shape
    lines = depth * rows
    dma = pltpu.SemaphoreType.DMA
    any_space = pl.BlockSpec(memory_space=pl.ANY)
    scalars = pl.BlockSpec(memory_space=pltpu.SMEM)
    return pl.pallas_call(
        kernel,
        out_shape=jax.ShapeDtypeStruct(courant.shape, F32),
        in_specs=[any_space, any_space, any_space, scalars, scalars],
        out_specs=pl.BlockSpec(memory_space=pltpu.VMEM),
        scratch_shapes=[
            pltpu.VMEM((256, 256), BF16), pltpu.VMEM((OFFSETS, 256, 256), BF16), pltpu.VMEM((4, 64, 256), F32), dma((3,)),
            pltpu.VMEM((16, 16, 256), BF16), pltpu.VMEM((16, 16, 256), BF16), dma((16,)), dma((16,)),
            pltpu.VMEM((16, OFFSETS, 16, 256), BF16), pltpu.VMEM((16, OFFSETS, 16, 256), BF16),
            dma((CHUNKS, 16)), dma((CHUNKS, 16)), dma,
            pltpu.VMEM((8, 128), jnp.int32), pltpu.VMEM((16, 8, 128), jnp.int32), pltpu.SMEM((16, 8, 128), jnp.int32),
            dma((16,)), dma((16,)), dma,
            pltpu.VMEM((4, 16, 128), F32), pltpu.VMEM((16, 128), F32), pltpu.VMEM((4, 16, 128), F32), dma((4,)), dma((4,)),
            pltpu.VMEM((4, 128, 128), BF16), pltpu.VMEM((3, 128, 128), BF16), dma((3,)), dma((3,)),
            pltpu.VMEM((128, 128), BF16), pltpu.VMEM((4, 128, 128), BF16), dma((4,)), dma((4,)),
            pltpu.VMEM((128, 128), F32), pltpu.VMEM((4, 64, 128), F32), dma((3,)), dma((3,)),
            pltpu.VMEM((2 * LAG + 1, 128, 256), F32),
            pltpu.VMEM((4, 128, 128), F32), pltpu.VMEM((3, 128, 128), F32), dma((2, 3)), dma((2, 3)),
            pltpu.VMEM((ROUNDS, 2, 16, 128), F32), pltpu.VMEM((ROUNDS, 4, 2, 16, 128), F32),
            pltpu.VMEM((ROUNDS - 1, len(FAR), 16, 128), F32), dma((ROUNDS, len(NEAR))), dma((ROUNDS, len(NEAR))),
            pltpu.VMEM((4, 8, 128), F32), dma((3,)), dma((3,)),
            pltpu.VMEM((16, 16, 256), F32), dma((16,)), dma((16,)),
        ],
        compiler_params=pltpu.CompilerParams(
            collective_id=0, has_side_effects=True, vmem_limit_bytes=60 * 1024 * 1024
        ),
        name="born",
    )(
        snapshots.reshape(lines, columns),
        reflect.reshape(reflect.shape[0], lines, columns),
        courant,
        lags,
        owners,
    )


def solution(mesh):
    in_specs = (
        P("off", "dep", None, None),
        P("off", "dep", None, None),
        P("dep", None, None),
        P("off"),
        P(),
    )
    return jax.shard_map(
        per_device, mesh=mesh, in_specs=in_specs, out_specs=P("dep", None, None), check_vma=False
    )
```

time: 105 us -> 101 us (0.962)
  local copies, waits for them, and re-layouts: 5.28 us -> 1.67 us
    unnamed x11 -> x1, local copies, waits for them, and re-layouts: 5.28 us -> 1.67 us
where the time goes in v2:
time: 101 us
  Pallas kernels  99.6 us (99%)
  local copies, waits for them, and re-layouts  1.67 us (2%)
    pallas_call x1, Pallas kernels, per_device(): pl.pallas_call(kernel, out_shape=jax.ShapeDtypeStruct(courant.shape, F32)...  99.6 us

profile of v2, /device:TPU:1, one launch (start us, length us, event | category | flops | bytes accessed | tf_op | source)
XLA Modules:
  0.0 101.3 jit_solution(12656099190242420525)
XLA Ops:
  0.0 99.6 %born.1 = f32[4,64,256]{2,1,0:T(8,128)} custom-call(bf16[256,256]{1,0:T(8,128)(2,1)} %bitcast.3, bf16[12,256,256]{2,1,0:T(8,128)(2,1)} %bitcast.2, f32[4,64,256]{2,1,0:T(8,128)} %cour_hbm.1, s32[12]{0:T(128)} %lags_ref.1, s32[8]{0:T(128)} %owners_ref.1), custom_call_target="tpu_custom_call" | custom-call | tf_op jit(solution)/shard_map/born/pallas_call | solution.py:425
  99.7 1.7 %copy.7 = f32[4,64,256]{2,1,0:T(8,128)} copy(f32[4,64,256]{2,1,0:T(8,128)} %born.1) | data formatting | bytes 524288

commit v3 on v2

--- a/solution.py
+++ b/solution.py
@@ -14,7 +14,7 @@
 OFFSETS = 12
 CHUNKS = 3
 PART = OFFSETS // CHUNKS
-FIRST = 3
+FIRST = 2
 STAR = ((-1, 0), (1, 0), (0, -1), (0, 1))
 FAR = ((-2, 0), (2, 0), (0, -2), (0, 2), (-1, -1), (-1, 1), (1, -1), (1, 1))
 NEAR = STAR + FAR
@@ -34,33 +34,57 @@
     return 4 * y + x + rem(y, 2) * (3 - 2 * x)
 
 
-def laplace(cur, prev, nxt, up, down):
+def inner(cur):
     row = lax.broadcasted_iota(jnp.int32, (8, 128), 0)
     line = rem(row, 4)
-    halves = lambda v: (v[:8], v[8:])
-    turned = lambda v: pltpu.roll(v, 4, 0)
-    (u0, u1), (c0, c1), (d0, d1) = halves(up), halves(cur), halves(down)
-    tu0, tu1, tc0, tc1, td0, td1 = [turned(v) for v in (u0, u1, c0, c1, d0, d1)]
-    join = lambda a, b: jnp.where(row < 4, a, b)
-    uu, uc, cc, cd, dd = join(tu0, tu1), join(tu1, tc0), join(tc0, tc1), join(tc1, td0), join(td0, td1)
+    c0, c1 = cur[:8], cur[8:]
+    t0, t1 = pltpu.roll(c0, 4, 0), pltpu.roll(c1, 4, 0)
+    both = jnp.where(row < 4, t0, t1)
     depth = (
-        {1: cc + uc, 2: c1 + u1, 3: cd + uu, 4: d0 + u0},
-        {1: cd + cc, 2: d0 + c0, 3: dd + uc, 4: d1 + u1},
+        {1: both + jnp.where(row < 4, 0.0, t0), 2: c1, 3: jnp.where(row < 4, t1, 0.0)},
+        {1: both + jnp.where(row < 4, t1, 0.0), 2: c0, 3: jnp.where(row < 4, 0.0, t0)},
     )
     out = []
-    for half in range(2):
-        c, p, n = halves(cur)[half], halves(prev)[half], halves(nxt)[half]
+    for half, c in enumerate((c0, c1)):
         total = (3.0 * WEIGHTS[0]) * c
         for k in range(1, 5):
-            near = depth[half][k] + pltpu.roll(c, 128 - k, 1) + pltpu.roll(c, k, 1)
+            near = pltpu.roll(c, 128 - k, 1) + pltpu.roll(c, k, 1)
             if k < 4:
-                near = near + jnp.where(line < 4 - k, pltpu.roll(c, 8 - k, 0), pltpu.roll(n, 4 - k, 0))
-                near = near + jnp.where(line >= k, pltpu.roll(c, k, 0), pltpu.roll(p, 4 + k, 0))
-            else:
-                near = near + n + p
+                near = near + depth[half][k]
+                near = near + jnp.where(line < 4 - k, pltpu.roll(c, 8 - k, 0), 0.0)
+                near = near + jnp.where(line >= k, pltpu.roll(c, k, 0), 0.0)
             total = total + WEIGHTS[k] * near
         out.append(total)
     return jnp.concatenate(out, axis=0)
+
+
+def rim(side, tile):
+    row = lax.broadcasted_iota(jnp.int32, (8, 128), 0)
+    line = rem(row, 4)
+    w = WEIGHTS
+    a, b = tile[:8], tile[8:]
+    if side[1] == 0:
+        out = []
+        for v in (a, b):
+            total = w[4] * v
+            for k in range(1, 4):
+                if side[0] > 0:
+                    total = total + w[k] * jnp.where(line < 4 - k, 0.0, pltpu.roll(v, 4 - k, 0))
+                else:
+                    total = total + w[k] * jnp.where(line < k, pltpu.roll(v, 4 + k, 0), 0.0)
+            out.append(total)
+        return jnp.concatenate(out, axis=0)
+    ta, tb = pltpu.roll(a, 4, 0), pltpu.roll(b, 4, 0)
+    both = jnp.where(row < 4, ta, tb)
+    if side[1] > 0:
+        last = jnp.where(row < 4, 0.0, ta)
+        return jnp.concatenate(
+            [w[3] * last + w[4] * a, w[1] * last + w[2] * a + w[3] * both + w[4] * b], axis=0
+        )
+    first = jnp.where(row < 4, tb, 0.0)
+    return jnp.concatenate(
+        [w[1] * first + w[2] * b + w[3] * both + w[4] * a, w[3] * first + w[4] * b], axis=0
+    )
 
 
 def windows(field):
@@ -150,6 +174,7 @@
 
         lax.fori_loop(lower, upper, run, 0)
 
+    masks = {place: inside(place) for place in NEAR}
     barrier = pltpu.get_barrier_semaphore()
 
     def greet(to):
@@ -179,6 +204,13 @@
 
     loads[0].wait()
     snap_t[...] = ordered(snap_v[...])
+
+    loads[1].wait()
+
+    def order_one(h):
+        refl_t[:, pl.ds(h, 1)] = ordered(refl_v[h])[:, None]
+
+    each(0, PART, order_one)
 
     pl.semaphore_wait(barrier, 18 + len(met))
     def snap_copy(k, to, slot):
@@ -198,13 +230,9 @@
 
     each(1, 16, lambda k: snap_copy(k, column_ahead(k), xy).start())
     snap_r[pl.ds(xy, 1)] = snap_t[pl.ds(block, 1)]
-    loads[1].wait()
-
-    def order_one(h):
-        refl_t[:, pl.ds(h, 1)] = ordered(refl_v[h])[:, None]
-
     for part in range(CHUNKS):
-        each(part * PART, (part + 1) * PART, order_one)
+        if part:
+            each(part * PART, (part + 1) * PART, order_one)
         each(1, 16, lambda k: refl_copy(part, k, column_ahead(k), xy).start())
     each(1, 16, lambda k: lag_copy(k, column_ahead(k), xy).start())
     own = pltpu.make_async_copy(refl_t.at[block], refl_r.at[xy], own_sem)
@@ -247,17 +275,20 @@
     def back_copy(i):
         return remote(back_s, back_r.at[i], back_ss.at[i], back_rs.at[i], beside(against(STAR[i])))
 
-    for i in range(4):
+    for i in reversed(range(4)):
         back_copy(i).start()
     for i in range(4):
         back_copy(i).wait_recv()
 
-    def accelerate(t):
-        rows = pl.ds(pl.multiple_of(16 * t, 16), 16)
-        rim = [back_r[i, rows, :].astype(F32) * inside(STAR[i]) for i in range(4)]
-        acc_w[rows, :] = courant * laplace(back_s[rows, :].astype(F32), *rim)
-
-    each(0, ITERS, accelerate)
+    def accelerate(i):
+        for j in range(4):
+            rows = pl.ds(pl.multiple_of(64 * i + 16 * j, 16), 16)
+            total = inner(back_s[rows, :].astype(F32))
+            for n, side in enumerate(STAR):
+                total = total + rim(side, back_r[n, rows, :].astype(F32)) * masks[side]
+            acc_w[rows, :] = courant * total
+
+    each(0, ITERS // 4, accelerate)
     acc_z[pl.ds(z, 1)] = packed(acc_w[:64, :], acc_w[64:, :])[None]
     def acc_zcopy(k, slot):
         return remote(acc_z.at[slot], acc_z.at[slot], acc_zss.at[k - 1], acc_zrs.at[k - 1], in_column(rem(z + k, 4)))
@@ -266,46 +297,57 @@
         acc_zcopy(k, z).start()
     for k in range(1, 4):
         acc_zcopy(k, rem(z + 4 - k, 4)).wait_recv()
-    wide = lax.broadcasted_iota(jnp.int32, (64, 128), 1)
-    for side in range(2):
-        a = unpacked(acc_z[0], acc_z[1])[side]
-        b = unpacked(acc_z[2], acc_z[3])[side]
-        rows = slice(64 * side, 64 * side + 64)
-
-        def move_right(lag):
-            ra, rb = pltpu.roll(a, lag, 1), pltpu.roll(b, lag, 1)
-            moved[LAG + lag, rows, :128] = jnp.where(wide < lag, 0.0, ra)
-            moved[LAG + lag, rows, 128:] = jnp.where(wide < lag, ra, rb)
-
-        def move_left(lag):
-            ra, rb = pltpu.roll(a, 128 - lag, 1), pltpu.roll(b, 128 - lag, 1)
-            moved[LAG - lag, rows, :128] = jnp.where(wide < 128 - lag, ra, rb)
-            moved[LAG - lag, rows, 128:] = jnp.where(wide < 128 - lag, rb, 0.0)
-
-        each(0, LAG + 1, move_right)
-        each(1, LAG + 1, move_left)
+    first = jnp.concatenate(unpacked(acc_z[0], acc_z[1]), axis=0)
+    second = jnp.concatenate(unpacked(acc_z[2], acc_z[3]), axis=0)
+
+    def move_all(rows, unrolled):
+        a, b = first[rows], second[rows]
+        wide = lax.broadcasted_iota(jnp.int32, a.shape, 1)
+        moved[LAG, rows, :128] = a
+        moved[LAG, rows, 128:] = b
+
+        def move(i):
+            for j in range(1, unrolled + 1):
+                lag = unrolled * i + j
+                ra, rb = pltpu.roll(a, lag, 1), pltpu.roll(b, lag, 1)
+                moved[LAG + lag, rows, :128] = jnp.where(wide < lag, 0.0, ra)
+                moved[LAG + lag, rows, 128:] = jnp.where(wide < lag, ra, rb)
+                rest = 128 - lag
+                ra, rb = pltpu.roll(a, rest, 1), pltpu.roll(b, rest, 1)
+                moved[LAG - lag, rows, :128] = jnp.where(wide < rest, ra, rb)
+                moved[LAG - lag, rows, 128:] = jnp.where(wide < rest, rb, 0.0)
+
+        each(0, LAG // unrolled, move)
+
+    def add_parts(steps, ready):
+        sums = tuple(jnp.zeros((16, 256), F32) for _ in steps)
+        for part in range(CHUNKS):
+            ready(part)
+
+            def add_device(s, sums):
+                sums = list(sums)
+                for h in range(part * PART, (part + 1) * PART):
+                    image = refl_r[s, h].astype(F32)
+                    place = lag_s[s, 0, h] + LAG
+                    for i, t in enumerate(steps):
+                        sums[i] = sums[i] + image * moved[place, 16 * t : 16 * t + 16, :]
+                return tuple(sums)
+
+            sums = lax.fori_loop(0, 16, add_device, sums)
+        for i, t in enumerate(steps):
+            for q, window in enumerate(windows(sums[i])):
+                sum_s[q, 16 * t : 16 * t + 16, :] = window
+
+    def arrive(part):
+        each(1, 16, lambda k: refl_copy(part, k, xy, column_behind(k)).wait_recv())
+
     own.wait()
     each(1, 16, lambda k: lag_copy(k, xy, column_behind(k)).wait_recv())
     scalars = pltpu.make_async_copy(lag_r, lag_s, lag_sem)
     scalars.start()
     scalars.wait()
-    sums = tuple(jnp.zeros((16, 256), F32) for _ in range(ITERS))
-    for part in range(CHUNKS):
-        each(1, 16, lambda k: refl_copy(part, k, xy, column_behind(k)).wait_recv())
-
-        def add_device(s, sums):
-            sums = list(sums)
-            for h in range(part * PART, (part + 1) * PART):
-                image = refl_r[s, h].astype(F32)
-                place = lag_s[s, 0, h] + LAG
-                for t in range(ITERS):
-                    sums[t] = sums[t] + image * moved[place, 16 * t : 16 * t + 16, :]
-            return tuple(sums)
-
-        sums = lax.fori_loop(0, 16, add_device, sums)
-    for t in range(ITERS):
-        for q, window in enumerate(windows(sums[t])):
-            sum_s[q, 16 * t : 16 * t + 16, :] = window
+    move_all(slice(0, 16 * FIRST), 8)
+    add_parts(range(FIRST), arrive)
     spans = ((0, 16 * FIRST), (16 * FIRST, 16 * (ITERS - FIRST)))
 
     def sum_copy(i, k):
@@ -315,9 +357,23 @@
             sum_s.at[z_to, rows, :], sum_r.at[k - 1, rows, :], sum_ss.at[i, k - 1], sum_rs.at[i, k - 1], in_column(z_to)
         )
 
-    for i in range(2):
-        for k in range(1, 4):
-            sum_copy(i, k).start()
+    for k in range(1, 4):
+        sum_copy(0, k).start()
+    move_all(slice(16 * FIRST, 16 * ITERS), 4)
+    add_parts(range(FIRST, ITERS), lambda part: None)
+    for k in range(1, 4):
+        sum_copy(1, k).start()
+
+    each(1, 16, lambda k: snap_copy(k, column_ahead(k), xy).wait_send())
+    each(1, 16, lambda k: lag_copy(k, column_ahead(k), xy).wait_send())
+    for part in range(CHUNKS):
+        each(1, 16, lambda k: refl_copy(part, k, column_ahead(k), xy).wait_send())
+    for k in range(1, 4):
+        pick_copy(k).wait_send()
+        acc_zcopy(k, z).wait_send()
+    for i in range(4):
+        back_copy(i).wait_send()
+        cour_copy(i).wait_send()
     for k in range(1, 4):
         sum_copy(0, k).wait_recv()
 
@@ -340,38 +396,52 @@
     def at(a, b):
         return (a[0] + b[0], a[1] + b[1])
 
-    old = {place: jnp.zeros((16, 128), F32) for place in ((0, 0),) + STAR}
+    here = (0, 0)
+    old = {place: jnp.zeros((16, 128), F32) for place in (here,) + STAR}
     wave = source(0)
-    masks = {place: inside(place) for place in NEAR}
-    courants = {(0, 0): courant}
+    courants = {here: courant}
     for i, place in enumerate(STAR):
-        courants[place] = cour_r[i]
+        courants[place] = cour_r[i] * masks[place]
     for r in range(ROUNDS):
+        more = r < ROUNDS - 1
         wave_s[r, 0] = wave
-        if r == 1:
+        now = source(2 * r + 1)
+        if more:
+            wave_s[r, 1] = now
+        for i in reversed(sent(r)):
+            wave_copy(r, i).start()
+        if r:
+            for i in sent(r - 1):
+                wave_copy(r - 1, i).wait_send()
+        slope = {here: inner(wave)}
+        base = {here: 2.0 * wave - old[here] + now}
+        if more:
+            for side in STAR:
+                slope[side] = rim(against(side), wave)
+        for i in (0, 1, 4, 5, 2, 3, 6, 7, 8, 9, 10, 11):
+            if i not in sent(r):
+                continue
+            wave_copy(r, i).wait_recv()
+            place = NEAR[i]
+            tile = (wave_r[r, i, 0] if i < 4 else wave_f[r, i - 4]) * masks[place]
+            for side in STAR:
+                to = at(place, against(side))
+                if to in slope and (to != place) and (more or to == here):
+                    slope[to] = slope[to] + rim(side, tile)
+            if i < 4 and more:
+                slope[place] = slope[place] + inner(tile)
+                base[place] = 2.0 * tile - old[place] + wave_r[r, i, 1] * masks[place]
+        ahead = {place: base[place] + courants[place] * slope[place] for place in base}
+        if not more:
+            wave = ahead[here]
+            break
+        if r == 0:
             for k in range(1, 4):
                 sum_copy(1, k).wait_recv()
-        now = source(2 * r + 1)
-        if r < ROUNDS - 1:
-            wave_s[r, 1] = now
-        for i in sent(r):
-            wave_copy(r, i).start()
-        field = {(0, 0): wave}
-        for i in sent(r):
-            wave_copy(r, i).wait_recv()
-            place = NEAR[i]
-            field[place] = (wave_r[r, i, 0] if i < 4 else wave_f[r, i - 4]) * masks[place]
-        ahead = {}
-        for place in ((0, 0),) + (STAR if r < ROUNDS - 1 else ()):
-            rim = [field[at(place, side)] for side in STAR]
-            term = now if place == (0, 0) else wave_r[r, STAR.index(place), 1]
-            value = 2.0 * field[place] - old[place] + courants[place] * laplace(field[place], *rim) + term
-            ahead[place] = value if place == (0, 0) else value * masks[place]
-        if r == ROUNDS - 1:
-            wave = ahead[(0, 0)]
-            break
-        rim = [ahead[side] for side in STAR]
-        wave = 2.0 * ahead[(0, 0)] - wave + courant * laplace(ahead[(0, 0)], *rim) + source(2 * r + 2)
+        total = inner(ahead[here])
+        for side in STAR:
+            total = total + rim(side, ahead[side])
+        wave = 2.0 * ahead[here] - wave + courant * total + source(2 * r + 2)
         old = ahead
     last_z[pl.ds(z, 1)] = packed(wave[:8], wave[8:])[None]
 
@@ -397,22 +467,12 @@
             out_ref[layer, 8 * pair : 8 * pair + 8, :] = jnp.concatenate(
                 [last[2 * pair + i, 4 * layer : 4 * layer + 4, :] for i in range(2)], axis=0
             )
-    each(1, 16, lambda k: snap_copy(k, column_ahead(k), xy).wait_send())
-    each(1, 16, lambda k: lag_copy(k, column_ahead(k), xy).wait_send())
-    for part in range(CHUNKS):
-        each(1, 16, lambda k: refl_copy(part, k, column_ahead(k), xy).wait_send())
-    for k in range(1, 4):
-        pick_copy(k).wait_send()
-        acc_zcopy(k, z).wait_send()
+    for k in range(1, 4):
         sum_copy(0, k).wait_send()
         sum_copy(1, k).wait_send()
         last_zcopy(k, z).wait_send()
-    for i in range(4):
-        back_copy(i).wait_send()
-        cour_copy(i).wait_send()
-    for r in range(ROUNDS):
-        for i in sent(r):
-            wave_copy(r, i).wait_send()
+    for i in sent(ROUNDS - 1):
+        wave_copy(ROUNDS - 1, i).wait_send()
     each(1, 16, lambda k: last_copy(k, column_ahead(k), xy).wait_send())
 
 

time: 101 us -> 89.9 us (0.89)
  Pallas kernels: 99.6 us -> 88.1 us
    pallas_call x1, Pallas kernels: 99.6 us -> 88.1 us  [per_device(): pl.pallas_call(kernel, out_shape=jax.ShapeDtypeStruct(courant.shape, F32)...]
where the time goes in v3:
time: 89.9 us; the launch traced here: 89.8 us
  Pallas kernels  88.1 us (98%)
  local copies, waits for them, and re-layouts  1.67 us (2%)
    pallas_call x1, Pallas kernels, per_device(): pl.pallas_call(kernel, out_shape=jax.ShapeDtypeStruct(courant.shape, F32)...  88.1 us

profile of v3, /device:TPU:1, one launch (start us, length us, event | category | flops | bytes accessed | tf_op | source)
XLA Modules:
  0.0 89.8 jit_solution(10416255983293813127)
XLA Ops:
  0.0 88.1 %born.1 = f32[4,64,256]{2,1,0:T(8,128)} custom-call(bf16[256,256]{1,0:T(8,128)(2,1)} %bitcast.3, bf16[12,256,256]{2,1,0:T(8,128)(2,1)} %bitcast.2, f32[4,64,256]{2,1,0:T(8,128)} %cour_hbm.1, s32[12]{0:T(128)} %lags_ref.1, s32[8]{0:T(128)} %owners_ref.1), custom_call_target="tpu_custom_call" | custom-call | tf_op jit(solution)/shard_map/born/pallas_call | solution.py:485
  88.1 1.7 %copy.7 = f32[4,64,256]{2,1,0:T(8,128)} copy(f32[4,64,256]{2,1,0:T(8,128)} %born.1) | data formatting | bytes 524288

commit v4 on v3

--- a/solution.py
+++ b/solution.py
@@ -174,13 +174,17 @@
 
         lax.fori_loop(lower, upper, run, 0)
 
+    def every(body):
+        for k in range(1, 16):
+            body(jnp.int32(k))
+
     masks = {place: inside(place) for place in NEAR}
     barrier = pltpu.get_barrier_semaphore()
 
     def greet(to):
         pl.semaphore_signal(barrier, inc=1, device_id=to, device_id_type=MESH)
 
-    each(1, 16, lambda k: greet(in_plane(column_ahead(k))))
+    every(lambda k: greet(in_plane(column_ahead(k))))
     for k in range(1, 4):
         greet(in_column(rem(z + k, 4)))
     met = [place for place in NEAR if place[1] != 0]
@@ -228,15 +232,16 @@
             in_plane(to),
         )
 
-    each(1, 16, lambda k: snap_copy(k, column_ahead(k), xy).start())
+    every(lambda k: snap_copy(k, column_ahead(k), xy).start())
     snap_r[pl.ds(xy, 1)] = snap_t[pl.ds(block, 1)]
-    for part in range(CHUNKS):
+    def send_part(part):
         if part:
             each(part * PART, (part + 1) * PART, order_one)
-        each(1, 16, lambda k: refl_copy(part, k, column_ahead(k), xy).start())
-    each(1, 16, lambda k: lag_copy(k, column_ahead(k), xy).start())
-    own = pltpu.make_async_copy(refl_t.at[block], refl_r.at[xy], own_sem)
-    own.start()
+        every(lambda k: refl_copy(part, k, column_ahead(k), xy).start())
+
+    for part in (0, 1):
+        send_part(part)
+    every(lambda k: lag_copy(k, column_ahead(k), xy).start())
     loads[2].wait()
     odd = rem(block, 2)
     layers = []
@@ -253,7 +258,7 @@
 
     for i in range(4):
         cour_copy(i).start()
-    each(1, 16, lambda k: snap_copy(k, xy, column_behind(k)).wait_recv())
+    every(lambda k: snap_copy(k, xy, column_behind(k)).wait_recv())
     for t in range(ITERS):
         owner = owners_ref[t]
         kept = jnp.where(rem(owner, 4) == z, 1.0, 0.0).astype(F32)
@@ -277,6 +282,9 @@
 
     for i in reversed(range(4)):
         back_copy(i).start()
+    send_part(2)
+    own = pltpu.make_async_copy(refl_t.at[block], refl_r.at[xy], own_sem)
+    own.start()
     for i in range(4):
         back_copy(i).wait_recv()
 
@@ -339,20 +347,20 @@
                 sum_s[q, 16 * t : 16 * t + 16, :] = window
 
     def arrive(part):
-        each(1, 16, lambda k: refl_copy(part, k, xy, column_behind(k)).wait_recv())
+        every(lambda k: refl_copy(part, k, xy, column_behind(k)).wait_recv())
 
     own.wait()
-    each(1, 16, lambda k: lag_copy(k, xy, column_behind(k)).wait_recv())
+    every(lambda k: lag_copy(k, xy, column_behind(k)).wait_recv())
     scalars = pltpu.make_async_copy(lag_r, lag_s, lag_sem)
     scalars.start()
     scalars.wait()
     move_all(slice(0, 16 * FIRST), 8)
     add_parts(range(FIRST), arrive)
-    spans = ((0, 16 * FIRST), (16 * FIRST, 16 * (ITERS - FIRST)))
+    spans = ((0, FIRST), (FIRST, 1), (FIRST + 1, 2), (FIRST + 3, 2), (FIRST + 5, 1))
 
     def sum_copy(i, k):
         z_to = rem(z + k, 4)
-        rows = pl.ds(*spans[i])
+        rows = pl.ds(16 * spans[i][0], 16 * spans[i][1])
         return remote(
             sum_s.at[z_to, rows, :], sum_r.at[k - 1, rows, :], sum_ss.at[i, k - 1], sum_rs.at[i, k - 1], in_column(z_to)
         )
@@ -364,10 +372,10 @@
     for k in range(1, 4):
         sum_copy(1, k).start()
 
-    each(1, 16, lambda k: snap_copy(k, column_ahead(k), xy).wait_send())
-    each(1, 16, lambda k: lag_copy(k, column_ahead(k), xy).wait_send())
+    every(lambda k: snap_copy(k, column_ahead(k), xy).wait_send())
+    every(lambda k: lag_copy(k, column_ahead(k), xy).wait_send())
     for part in range(CHUNKS):
-        each(1, 16, lambda k: refl_copy(part, k, column_ahead(k), xy).wait_send())
+        every(lambda k: refl_copy(part, k, column_ahead(k), xy).wait_send())
     for k in range(1, 4):
         pick_copy(k).wait_send()
         acc_zcopy(k, z).wait_send()
@@ -410,6 +418,9 @@
             wave_s[r, 1] = now
         for i in reversed(sent(r)):
             wave_copy(r, i).start()
+        if more:
+            for k in range(1, 4):
+                sum_copy(2 + r, k).start()
         if r:
             for i in sent(r - 1):
                 wave_copy(r - 1, i).wait_send()
@@ -435,9 +446,9 @@
         if not more:
             wave = ahead[here]
             break
-        if r == 0:
+        for i in (1, 2) if r == 0 else (2 + r,):
             for k in range(1, 4):
-                sum_copy(1, k).wait_recv()
+                sum_copy(i, k).wait_recv()
         total = inner(ahead[here])
         for side in STAR:
             total = total + rim(side, ahead[side])
@@ -460,20 +471,20 @@
         place = snake(column)
         return remote(last.at[place], last.at[place], last_ss.at[k], last_rs.at[k], in_plane(to))
 
-    each(1, 16, lambda k: last_copy(k, column_ahead(k), xy).start())
-    each(1, 16, lambda k: last_copy(k, xy, column_behind(k)).wait_recv())
+    every(lambda k: last_copy(k, column_ahead(k), xy).start())
+    every(lambda k: last_copy(k, xy, column_behind(k)).wait_recv())
     for layer in range(4):
         for pair in range(8):
             out_ref[layer, 8 * pair : 8 * pair + 8, :] = jnp.concatenate(
                 [last[2 * pair + i, 4 * layer : 4 * layer + 4, :] for i in range(2)], axis=0
             )
     for k in range(1, 4):
-        sum_copy(0, k).wait_send()
-        sum_copy(1, k).wait_send()
+        for i in range(len(spans)):
+            sum_copy(i, k).wait_send()
         last_zcopy(k, z).wait_send()
     for i in sent(ROUNDS - 1):
         wave_copy(ROUNDS - 1, i).wait_send()
-    each(1, 16, lambda k: last_copy(k, column_ahead(k), xy).wait_send())
+    every(lambda k: last_copy(k, column_ahead(k), xy).wait_send())
 
 
 def per_device(snapshots, reflect, courant, lags, owners):
@@ -499,7 +510,7 @@
             pltpu.VMEM((128, 128), BF16), pltpu.VMEM((4, 128, 128), BF16), dma((4,)), dma((4,)),
             pltpu.VMEM((128, 128), F32), pltpu.VMEM((4, 64, 128), F32), dma((3,)), dma((3,)),
             pltpu.VMEM((2 * LAG + 1, 128, 256), F32),
-            pltpu.VMEM((4, 128, 128), F32), pltpu.VMEM((3, 128, 128), F32), dma((2, 3)), dma((2, 3)),
+            pltpu.VMEM((4, 128, 128), F32), pltpu.VMEM((3, 128, 128), F32), dma((5, 3)), dma((5, 3)),
             pltpu.VMEM((ROUNDS, 2, 16, 128), F32), pltpu.VMEM((ROUNDS, 4, 2, 16, 128), F32),
             pltpu.VMEM((ROUNDS - 1, len(FAR), 16, 128), F32), dma((ROUNDS, len(NEAR))), dma((ROUNDS, len(NEAR))),
             pltpu.VMEM((4, 8, 128), F32), dma((3,)), dma((3,)),

time: 89.9 us -> 83.3 us (0.927)
  Pallas kernels: 88.1 us -> 81.5 us
    pallas_call x1, Pallas kernels: 88.1 us -> 81.5 us  [per_device(): pl.pallas_call(kernel, out_shape=jax.ShapeDtypeStruct(courant.shape, F32)...]
where the time goes in v4:
time: 83.3 us; the launch traced here: 83.1 us
  Pallas kernels  81.5 us (98%)
  local copies, waits for them, and re-layouts  1.67 us (2%)
    pallas_call x1, Pallas kernels, per_device(): pl.pallas_call(kernel, out_shape=jax.ShapeDtypeStruct(courant.shape, F32)...  81.5 us
    unnamed x1, local copies, waits for them, and re-layouts  1.67 us

profile of v4, /device:TPU:1, one launch (start us, length us, event | category | flops | bytes accessed | tf_op | source)
XLA Modules:
  0.0 83.1 jit_solution(12956921571389471637)
XLA Ops:
  0.0 81.5 %born.1 = f32[4,64,256]{2,1,0:T(8,128)} custom-call(bf16[256,256]{1,0:T(8,128)(2,1)} %bitcast.3, bf16[12,256,256]{2,1,0:T(8,128)(2,1)} %bitcast.2, f32[4,64,256]{2,1,0:T(8,128)} %cour_hbm.1, s32[12]{0:T(128)} %lags_ref.1, s32[8]{0:T(128)} %owners_ref.1), custom_call_target="tpu_custom_call" | custom-call | tf_op jit(solution)/shard_map/born/pallas_call | solution.py:496
  81.5 1.7 %copy.7 = f32[4,64,256]{2,1,0:T(8,128)} copy(f32[4,64,256]{2,1,0:T(8,128)} %born.1) | data formatting | bytes 524288

commit v5 on v4

--- a/solution.py
+++ b/solution.py
@@ -12,7 +12,7 @@
 F32 = jnp.float32
 BF16 = jnp.bfloat16
 OFFSETS = 12
-CHUNKS = 3
+CHUNKS = 4
 PART = OFFSETS // CHUNKS
 FIRST = 2
 STAR = ((-1, 0), (1, 0), (0, -1), (0, 1))
@@ -121,7 +121,7 @@
     back_s, back_r, back_ss, back_rs,
     acc_w, acc_z, acc_zss, acc_zrs, moved,
     sum_s, sum_r, sum_ss, sum_rs,
-    wave_s, wave_r, wave_f, wave_ss, wave_rs,
+    wave_s, wave_r, wave_f, wave_ss, wave_rs, term_ss, term_rs,
     last_z, last_zss, last_zrs,
     last, last_ss, last_rs,
 ):
@@ -283,8 +283,6 @@
     for i in reversed(range(4)):
         back_copy(i).start()
     send_part(2)
-    own = pltpu.make_async_copy(refl_t.at[block], refl_r.at[xy], own_sem)
-    own.start()
     for i in range(4):
         back_copy(i).wait_recv()
 
@@ -303,6 +301,9 @@
 
     for k in range(1, 4):
         acc_zcopy(k, z).start()
+    send_part(3)
+    own = pltpu.make_async_copy(refl_t.at[block], refl_r.at[xy], own_sem)
+    own.start()
     for k in range(1, 4):
         acc_zcopy(k, rem(z + 4 - k, 4)).wait_recv()
     first = jnp.concatenate(unpacked(acc_z[0], acc_z[1]), axis=0)
@@ -395,8 +396,12 @@
     def wave_copy(r, i):
         to = beside(against(NEAR[i]))
         if i < 4:
-            return remote(wave_s.at[r], wave_r.at[r, i], wave_ss.at[r, i], wave_rs.at[r, i], to)
+            return remote(wave_s.at[r, 0], wave_r.at[r, i, 0], wave_ss.at[r, i], wave_rs.at[r, i], to)
         return remote(wave_s.at[r, 0], wave_f.at[r, i - 4], wave_ss.at[r, i], wave_rs.at[r, i], to)
+
+    def term_copy(r, i):
+        to = beside(against(STAR[i]))
+        return remote(wave_s.at[r, 1], wave_r.at[r, i, 1], term_ss.at[r, i], term_rs.at[r, i], to)
 
     def sent(r):
         return range(len(NEAR) if r < ROUNDS - 1 else 4)
@@ -413,17 +418,22 @@
     for r in range(ROUNDS):
         more = r < ROUNDS - 1
         wave_s[r, 0] = wave
+        for i in (11, 10, 9, 8, 7, 6, 3, 2, 5, 4, 1, 0):
+            if i in sent(r):
+                wave_copy(r, i).start()
         now = source(2 * r + 1)
         if more:
             wave_s[r, 1] = now
-        for i in reversed(sent(r)):
-            wave_copy(r, i).start()
+            for i in (3, 2, 1, 0):
+                term_copy(r, i).start()
         if more:
             for k in range(1, 4):
                 sum_copy(2 + r, k).start()
         if r:
             for i in sent(r - 1):
                 wave_copy(r - 1, i).wait_send()
+            for i in range(4):
+                term_copy(r - 1, i).wait_send()
         slope = {here: inner(wave)}
         base = {here: 2.0 * wave - old[here] + now}
         if more:
@@ -441,7 +451,10 @@
                     slope[to] = slope[to] + rim(side, tile)
             if i < 4 and more:
                 slope[place] = slope[place] + inner(tile)
-                base[place] = 2.0 * tile - old[place] + wave_r[r, i, 1] * masks[place]
+                base[place] = 2.0 * tile - old[place]
+        for i in range(4 if more else 0):
+            term_copy(r, i).wait_recv()
+            base[STAR[i]] = base[STAR[i]] + wave_r[r, i, 1] * masks[STAR[i]]
         ahead = {place: base[place] + courants[place] * slope[place] for place in base}
         if not more:
             wave = ahead[here]
@@ -454,37 +467,48 @@
             total = total + rim(side, ahead[side])
         wave = 2.0 * ahead[here] - wave + courant * total + source(2 * r + 2)
         old = ahead
-    last_z[pl.ds(z, 1)] = packed(wave[:8], wave[8:])[None]
-
-    def last_zcopy(k, slot):
-        return remote(last_z.at[slot], last_z.at[slot], last_zss.at[k - 1], last_zrs.at[k - 1], in_column(rem(z + k, 4)))
-
-    for k in range(1, 4):
-        last_zcopy(k, z).start()
-    for k in range(1, 4):
-        last_zcopy(k, rem(z + 4 - k, 4)).wait_recv()
-    west, east = unpacked(last_z[0], last_z[1]), unpacked(last_z[2], last_z[3])
-    slab = jnp.concatenate([jnp.concatenate([west[i], east[i]], axis=1) for i in range(2)], axis=0)
-    last[pl.ds(block, 1)] = slab[None]
-
-    def last_copy(k, to, column):
-        place = snake(column)
-        return remote(last.at[place], last.at[place], last_ss.at[k], last_rs.at[k], in_plane(to))
-
-    every(lambda k: last_copy(k, column_ahead(k), xy).start())
-    every(lambda k: last_copy(k, xy, column_behind(k)).wait_recv())
-    for layer in range(4):
-        for pair in range(8):
-            out_ref[layer, 8 * pair : 8 * pair + 8, :] = jnp.concatenate(
-                [last[2 * pair + i, 4 * layer : 4 * layer + 4, :] for i in range(2)], axis=0
-            )
+    last_z[0] = packed(wave[:8], wave[8:])
+
+    def last_zcopy(k):
+        return remote(last_z.at[0], last_z.at[k], last_zss.at[k - 1], last_zrs.at[k - 1], in_column(rem(z + k, 4)))
+
+    def last_copy(i, k, to, column):
+        slots = pl.ds(0, 1) if i == 0 else pl.ds(1, 3)
+        return remote(last_z.at[slots], last.at[snake(column), slots], last_ss.at[i, k], last_rs.at[i, k], in_plane(to))
+
+    for k in range(1, 4):
+        last_zcopy(k).start()
+    every(lambda k: last_copy(0, k, column_ahead(k), xy).start())
     for k in range(1, 4):
         for i in range(len(spans)):
             sum_copy(i, k).wait_send()
-        last_zcopy(k, z).wait_send()
     for i in sent(ROUNDS - 1):
         wave_copy(ROUNDS - 1, i).wait_send()
-    every(lambda k: last_copy(k, column_ahead(k), xy).wait_send())
+    for k in range(1, 4):
+        last_zcopy(k).wait_recv()
+    every(lambda k: last_copy(1, k, column_ahead(k), xy).start())
+    last[pl.ds(block, 1)] = last_z[...][None]
+    every(lambda k: last_copy(0, k, xy, column_behind(k)).wait_recv())
+    every(lambda k: last_copy(1, k, xy, column_behind(k)).wait_recv())
+
+    def quarter(place, q):
+        return last[place, pl.ds(rem(z - q + 4, 4), 1)][0]
+
+    for pair in range(8):
+        slabs = []
+        for place in (2 * pair, 2 * pair + 1):
+            west = unpacked(quarter(place, 0), quarter(place, 1))
+            east = unpacked(quarter(place, 2), quarter(place, 3))
+            slabs.append([jnp.concatenate([west[half], east[half]], axis=1) for half in range(2)])
+        for layer in range(4):
+            rows = slice(4 * (layer % 2), 4 * (layer % 2) + 4)
+            out_ref[layer, 8 * pair : 8 * pair + 8, :] = jnp.concatenate(
+                [slab[layer // 2][rows] for slab in slabs], axis=0
+            )
+    for k in range(1, 4):
+        last_zcopy(k).wait_send()
+    for i in range(2):
+        every(lambda k: last_copy(i, k, column_ahead(k), xy).wait_send())
 
 
 def per_device(snapshots, reflect, courant, lags, owners):
@@ -513,8 +537,9 @@
             pltpu.VMEM((4, 128, 128), F32), pltpu.VMEM((3, 128, 128), F32), dma((5, 3)), dma((5, 3)),
             pltpu.VMEM((ROUNDS, 2, 16, 128), F32), pltpu.VMEM((ROUNDS, 4, 2, 16, 128), F32),
             pltpu.VMEM((ROUNDS - 1, len(FAR), 16, 128), F32), dma((ROUNDS, len(NEAR))), dma((ROUNDS, len(NEAR))),
+            dma((ROUNDS - 1, 4)), dma((ROUNDS - 1, 4)),
             pltpu.VMEM((4, 8, 128), F32), dma((3,)), dma((3,)),
-            pltpu.VMEM((16, 16, 256), F32), dma((16,)), dma((16,)),
+            pltpu.VMEM((16, 4, 8, 128), F32), dma((2, 16)), dma((2, 16)),
         ],
         compiler_params=pltpu.CompilerParams(
             collective_id=0, has_side_effects=True, vmem_limit_bytes=60 * 1024 * 1024

time: 83.3 us -> 82.4 us (0.989)
  Pallas kernels: 81.5 us -> 80.5 us
    pallas_call x1, Pallas kernels: 81.5 us -> 80.5 us  [per_device(): pl.pallas_call(kernel, out_shape=jax.ShapeDtypeStruct(courant.shape, F32)...]
where the time goes in v5:
time: 82.4 us; the launch traced here: 82.2 us
  Pallas kernels  80.5 us (98%)
  local copies, waits for them, and re-layouts  1.67 us (2%)
    pallas_call x1, Pallas kernels, per_device(): pl.pallas_call(kernel, out_shape=jax.ShapeDtypeStruct(courant.shape, F32)...  80.5 us
    unnamed x1, local copies, waits for them, and re-layouts  1.67 us

profile of v5, /device:TPU:1, one launch (start us, length us, event | category | flops | bytes accessed | tf_op | source)
XLA Modules:
  0.0 82.2 jit_solution(7726548597198218684)
XLA Ops:
  0.0 80.5 %born.1 = f32[4,64,256]{2,1,0:T(8,128)} custom-call(bf16[256,256]{1,0:T(8,128)(2,1)} %bitcast.3, bf16[12,256,256]{2,1,0:T(8,128)(2,1)} %bitcast.2, f32[4,64,256]{2,1,0:T(8,128)} %cour_hbm.1, s32[12]{0:T(128)} %lags_ref.1, s32[8]{0:T(128)} %owners_ref.1), custom_call_target="tpu_custom_call" | custom-call | tf_op jit(solution)/shard_map/born/pallas_call | solution.py:520
  80.5 1.7 %copy.7 = f32[4,64,256]{2,1,0:T(8,128)} copy(f32[4,64,256]{2,1,0:T(8,128)} %born.1) | data formatting | bytes 524288

commit v6 on v5

--- a/solution.py
+++ b/solution.py
@@ -294,7 +294,8 @@
                 total = total + rim(side, back_r[n, rows, :].astype(F32)) * masks[side]
             acc_w[rows, :] = courant * total
 
-    each(0, ITERS // 4, accelerate)
+    for i in range(ITERS // 4):
+        accelerate(i)
     acc_z[pl.ds(z, 1)] = packed(acc_w[:64, :], acc_w[64:, :])[None]
     def acc_zcopy(k, slot):
         return remote(acc_z.at[slot], acc_z.at[slot], acc_zss.at[k - 1], acc_zrs.at[k - 1], in_column(rem(z + k, 4)))

time: 82.4 us -> 82.8 us (level)
  no operation moved by 1% of the time
where the time goes in v6:
time: 82.8 us; the launch traced here: 82.6 us
  Pallas kernels  80.9 us (98%)
  local copies, waits for them, and re-layouts  1.67 us (2%)
    pallas_call x1, Pallas kernels, per_device(): pl.pallas_call(kernel, out_shape=jax.ShapeDtypeStruct(courant.shape, F32)...  80.9 us
    unnamed x1, local copies, waits for them, and re-layouts  1.67 us

profile of v6, /device:TPU:1, one launch (start us, length us, event | category | flops | bytes accessed | tf_op | source)
XLA Modules:
  0.0 82.6 jit_solution(13359662278419948898)
XLA Ops:
  0.0 80.9 %born.1 = f32[4,64,256]{2,1,0:T(8,128)} custom-call(bf16[256,256]{1,0:T(8,128)(2,1)} %bitcast.3, bf16[12,256,256]{2,1,0:T(8,128)(2,1)} %bitcast.2, f32[4,64,256]{2,1,0:T(8,128)} %cour_hbm.1, s32[12]{0:T(128)} %lags_ref.1, s32[8]{0:T(128)} %owners_ref.1), custom_call_target="tpu_custom_call" | custom-call | tf_op jit(solution)/shard_map/born/pallas_call | solution.py:521
  80.9 1.7 %copy.7 = f32[4,64,256]{2,1,0:T(8,128)} copy(f32[4,64,256]{2,1,0:T(8,128)} %born.1) | data formatting | bytes 524288
